TPU v7x, 32 devices: a whole 2x2x4 slice. The times are simulated.
32 devices in a mesh: chan: 2 (over x), elem: 2 (over y), beam: 8 (over z, core).
Axes of the slice: x: 2, y: 2, z: 4, core: 2. Of those that a mesh axis runs over, the one named last changes fastest.
Arguments:
- voltages: bfloat16 [2, 128, 128, 2048], P(None, 'chan', 'beam', 'elem'), may hold values from -6 to 6
- weights: bfloat16 [2, 128, 2048, 2048], P(None, 'chan', 'elem', 'beam'), may hold values from -0.09375 to 0.09375
Outputs:
- power: float32 [128, 128, 2048], P(None, ('chan', 'elem'), 'beam')
All inputs are finite; a program needn't handle non-finite values.
Results may differ from a plain program's by a relative error of at most 0.012.
Values may be sent and summed in bfloat16 or wider, within the bound.
No kernel may reach another device: no remote copies, remote signals or barrier semaphores. Data moves between devices by JAX's collectives and lax.ppermute only.
A program may use at most 192 MiB of HBM per device.

v0:
```python
import jax
import jax.numpy as jnp
from jax import lax
from jax.sharding import PartitionSpec as P


def dft_tables(channels):
    index = jnp.arange(channels, dtype=jnp.int32)
    phase = index[:, None] * index[None, :] % channels
    angle = phase.astype(jnp.float32) * (2.0 * jnp.pi / channels)
    factor = 1.0 / jnp.sqrt(jnp.float32(channels))
    return (jnp.cos(angle) * factor, jnp.sin(angle) * factor)


def shards(voltages, weights):
    local_channels = weights.shape[1]
    local_beams = weights.shape[3]
    volt_piece = lax.all_gather(voltages, "beam", axis=2, tiled=True)
    real_part = jnp.einsum(
        "cte,ceb->ctb", volt_piece[0], weights[0], preferred_element_type=jnp.float32
    ) - jnp.einsum("cte,ceb->ctb", volt_piece[1], weights[1], preferred_element_type=jnp.float32)
    imag_part = jnp.einsum(
        "cte,ceb->ctb", volt_piece[0], weights[1], preferred_element_type=jnp.float32
    ) + jnp.einsum("cte,ceb->ctb", volt_piece[1], weights[0], preferred_element_type=jnp.float32)
    partial_value = jnp.stack([real_part, imag_part])
    all_time = partial_value.shape[2]
    groups = lax.axis_size("chan")
    halves = partial_value.reshape(2, local_channels, groups, all_time // groups, local_beams)
    summed = lax.psum_scatter(halves.astype(jnp.bfloat16), "elem", scatter_dimension=3, tiled=True)
    owned = lax.all_to_all(summed, "chan", split_axis=2, concat_axis=1, tiled=True)
    owned = owned.reshape(2, owned.shape[1], owned.shape[3], local_beams)
    channels = owned.shape[1]
    own_time = owned.shape[2]
    cosine, sine = dft_tables(channels)
    real_in = owned[0].astype(jnp.float32).reshape(channels, own_time * local_beams)
    imag_in = owned[1].astype(jnp.float32).reshape(channels, own_time * local_beams)
    highest = lax.Precision.HIGHEST
    real_out = jnp.dot(
        cosine, real_in, precision=highest, preferred_element_type=jnp.float32
    ) - jnp.dot(sine, imag_in, precision=highest, preferred_element_type=jnp.float32)
    imag_out = jnp.dot(
        sine, real_in, precision=highest, preferred_element_type=jnp.float32
    ) + jnp.dot(cosine, imag_in, precision=highest, preferred_element_type=jnp.float32)
    power = real_out * real_out + imag_out * imag_out
    return power.reshape(channels, own_time, local_beams)


def solution(mesh):
    placed = (P(None, "chan", "beam", "elem"), P(None, "chan", "elem", "beam"))
    return jax.shard_map(
        shards,
        mesh=mesh,
        in_specs=placed,
        out_specs=P(None, ("chan", "elem"), "beam"),
        check_vma=False,
    )
```

profile of v0, /device:TPU:0, one launch (start us, length us, event | category | flops | bytes accessed | tf_op | source)
XLA Modules:
  0.0 574.3 jit_solution(12547224405652226396)
XLA Ops:
  6.5 0.0 all-gather.2.cloned.1.call-start
  6.5 0.7 all-gather.2.cloned.1.call-update
  7.3 0.0 reduce-scatter.2.cloned.1.call-start
  7.3 293.0 %all-gather.2.cloned.1.call-done = bf16[2,64,128,1024]{3,2,1,0:T(8,128)(2,1)} async-done(((bf16[2,64,16,1024]{3,2,1,0:T(8,128)(2,1)}), bf16[2,64,128,1024]{3,2,1,0:T(8,128)(2,1)}) %all-gather.2.cloned.1.call-update) | async-done | bytes 33554448 | tf_op jit(solution)/shard_map/all_gather | solution.py:18
  300.3 20.6 %fusion = f32[64,128,256]{2,1,0:T(8,128)} fusion(bf16[2,64,1024,256]{3,2,1,0:T(8,128)(2,1)} %param.3, bf16[2,64,128,1024]{3,2,1,0:T(8,128)(2,1)} %all-gather.2.cloned.1.call-done), kind=kOutput, calls=%fused_computation | convolution fusion | flops 4294967296 | bytes 58720256 | tf_op jit(solution)/shard_map/cte,ceb->ctb/dot_general | solution.py:22
  320.9 20.6 %fusion.2 = f32[64,128,256]{2,1,0:T(8,128)} fusion(bf16[2,64,1024,256]{3,2,1,0:T(8,128)(2,1)} %param.3, bf16[2,64,128,1024]{3,2,1,0:T(8,128)(2,1)} %all-gather.2.cloned.1.call-done), kind=kOutput, calls=%fused_computation.2 | convolution fusion | flops 4294967296 | bytes 58720256 | tf_op jit(solution)/shard_map/cte,ceb->ctb/dot_general | solution.py:21
  341.5 22.6 %add_convert_fusion = bf16[64,128,256]{2,1,0:T(8,128)(2,1)} fusion(f32[64,128,256]{2,1,0:T(8,128)} %fusion, bf16[2,64,1024,256]{3,2,1,0:T(8,128)(2,1)} %param.3, bf16[2,64,128,1024]{3,2,1,0:T(8,128)(2,1)} %all-gather.2.cloned.1.call-done), kind=kOutput, calls=%fused_computation.20 | convolution fusion | flops 4299161600 | bytes 62914560 | tf_op jit(solution)/shard_map/cte,ceb->ctb/dot_general | solution.py:24
  364.1 22.6 %subtract_convert_fusion = bf16[64,128,256]{2,1,0:T(8,128)(2,1)} fusion(f32[64,128,256]{2,1,0:T(8,128)} %fusion.2, bf16[2,64,1024,256]{3,2,1,0:T(8,128)(2,1)} %param.3, bf16[2,64,128,1024]{3,2,1,0:T(8,128)(2,1)} %all-gather.2.cloned.1.call-done), kind=kOutput, calls=%fused_computation.21 | convolution fusion | flops 4299161600 | bytes 62914560 | tf_op jit(solution)/shard_map/cte,ceb->ctb/dot_general | solution.py:19
  386.6 7.4 %pad_maximum_fusion = bf16[2,64,2,64,256]{4,3,2,1,0:T(8,128)(2,1)} fusion(bf16[1,64,2,64,256]{4,3,2,1,0:T(8,128)(2,1)} %bitcast.53, bf16[1,64,2,64,256]{4,3,2,1,0:T(8,128)(2,1)} %bitcast.54), kind=kLoop, calls=%fused_computation.19 | loop fusion | flops 4194304 | bytes 16777216 | tf_op jit(solution)/shard_map/stack | solution.py:25
  394.1 8.3 %copy.7 = bf16[2,64,2,64,256]{4,3,1,0,2:T(8,128)(2,1)} copy(bf16[2,64,2,64,256]{4,3,2,1,0:T(8,128)(2,1)} %pad_maximum_fusion) | data formatting | bytes 16777216 | tf_op jit(solution)/shard_map/stack | solution.py:25
  402.3 0.0 reduce-scatter.2.cloned.1.call-update
  402.3 97.6 %reduce-scatter.2.cloned.1.call-done = bf16[2,64,2,32,256]{4,3,1,0,2:T(8,128)(2,1)} async-done(((bf16[2,64,2,64,256]{4,3,1,0,2:T(8,128)(2,1)}), bf16[2,64,2,32,256]{4,3,1,0,2:T(8,128)(2,1)}) %reduce-scatter.2.cloned.1.call-update) | async-done | bytes 4194320 | tf_op jit(solution)/shard_map/reduce_scatter | solution.py:29
  499.9 51.7 %all_to_all.15 = bf16[2,64,2,32,256]{4,3,1,0,2:T(8,128)(2,1)S(1)} all-to-all(bf16[2,64,2,32,256]{4,3,1,0,2:T(8,128)(2,1)} %reduce-scatter.2.cloned.1.call-done), channel_id=1, replica_groups=mesh['chan'=2,'elem'=2,'beam'=8] {'chan'}, dimensions={2} | all-to-all | bytes 8388608 | tf_op jit(solution)/shard_map/all_to_all | solution.py:30
  551.6 0.4 fusion.55
  552.1 1.4 copy.8
  553.5 2.1 fusion.26
  555.6 2.0 fusion.25
  557.6 1.4 copy.9
  559.0 2.4 fusion.14
  561.4 2.7 fusion.13
  564.2 3.3 copy.10
Async XLA Ops:
  6.5 293.8 %all-gather.2.cloned.1.call-start = ((), (), s32[]{:S(2)}) async-start(), calls=%async_computation.2 | async-start | bytes 37748736 | tf_op jit(solution)/shard_map/all_gather | solution.py:18
  7.3 492.7 %reduce-scatter.2.cloned.1.call-start = ((), (), s32[]{:S(2)}) async-start(), calls=%async_computation.3 | async-start | bytes 12582912 | tf_op jit(solution)/shard_map/reduce_scatter | solution.py:29
Sparse Core Ops, SparseCore 0:
  9.0 291.3 all-gather.1
  402.5 97.4 reduce-scatter.1
where the time goes:
time: 575 us; the launch traced here: 574 us
  waiting for transfers between devices  391 us (68%)
  matrix products  95.5 us (17%)
  blocking collectives  51.7 us (9%)
  local copies, waits for them, and re-layouts  14.9 us (3%)
  between operations  13.4 us (2%)
  other arithmetic  7.45 us (1%)
    all_gather x1, waiting for transfers between devices, shards(): volt_piece = lax.all_gather(voltages, 'beam', axis=2, tiled=True)  293 us
    reduce_scatter x1, waiting for transfers between devices, shards(): lax.psum_scatter(halves.astype(jnp.bfloat16), 'elem', scatter_dimension=3...  97.6 us
    all_to_all x1, blocking collectives, shards(): lax.all_to_all(summed, 'chan', split_axis=2, concat_axis=1, tiled=True)  51.7 us
    dot_general x1, matrix products, shards(): jnp.einsum('cte,ceb->ctb', volt_piece[1], weights[0], preferred_element_t...  22.6 us
    dot_general x1, matrix products, shards(): jnp.einsum('cte,ceb->ctb', volt_piece[0], weights[0], preferred_element_t...  22.6 us
    dot_general x1, matrix products, shards(): jnp.einsum('cte,ceb->ctb', volt_piece[1], weights[1], preferred_element_t...  20.6 us
    dot_general x1, matrix products, shards(): jnp.einsum('cte,ceb->ctb', volt_piece[0], weights[1], preferred_element_t...  20.6 us
  transfers between devices with their start and end apart: 2, of which 2 were waited for; matrix products, arithmetic and copies ran while one was open for 0% of the time, Pallas kernels for 0%

commit v1 on v0

v1 whole, which is shorter than its diff:
```python
import functools
import math

import jax
import jax.numpy as jnp
from jax import lax
from jax.experimental import pallas as pl
from jax.experimental.pallas import tpu as pltpu
from jax.sharding import PartitionSpec as P

F32 = jnp.float32
BF16 = jnp.bfloat16
VMEM_BYTES = 40 * 2**20
WINDOW = (3,)
Y_LAG, X_LAG, RING_LAG, UNGATED = 1, 2, 0, 0
FLOPS = 32
CUTS = 2
GROUP = 4
PLAN = ((0, 6), (0, 6), (0, 6), (0, 6), (0, 4), (0, 2), (0, 2))


def groups_of_channels(channels):
    unit = channels // 32
    plan, first = [], 0
    for gathered, units in PLAN:
        plan.append((gathered, first, units * unit))
        first += units * unit
    return plan


def beamform_kernel(sizes, scalars, *refs):
    n, group, time, own, elems, chans, counts, slots = sizes
    halves, refs = refs[: 2 * CUTS], refs[2 * CUTS :]
    blocks, outs = refs[: len(counts)], refs[len(counts) : len(counts) + elems]
    volt, result = refs[len(counts) + elems :]
    step = pl.program_id(0)
    lanes = result.shape[2]
    for g in range(group):
        if blocks[0].shape[2] == time:
            held = blocks[0][:, g].reshape(2 * time, blocks[0].shape[3])
        else:
            slot = 0
            for ref, count in zip(blocks, counts):
                rows = ref.shape[2]
                for j in range(count):
                    at = pl.multiple_of(scalars[slot], rows)
                    volt[g, pl.ds(at, rows), :] = ref[2 * j, g]
                    volt[g, pl.ds(pl.multiple_of(time + at, rows), rows), :] = ref[2 * j + 1, g]
                    slot += 1
            held = volt[g]
        products = []
        for part in range(2):
            total = None
            for j, ref in enumerate(halves[part * CUTS : (part + 1) * CUTS]):
                depth = ref.shape[2]
                term = jnp.dot(held[:, j * depth : (j + 1) * depth], ref[0, g], preferred_element_type=F32)
                total = term if total is None else total + term
            products.append(total)
        by_real, by_imag = products
        real_part = by_real[:time] - by_imag[time:]
        imag_part = by_real[time:] + by_imag[:time]
        row = step * group + g
        for k in range(result.shape[0]):
            cut = slice(k * lanes, (k + 1) * lanes)
            result[k, pl.ds(row, time, stride=2 * n), :] = real_part[:, cut]
            result[k, pl.ds(n + row, time, stride=2 * n), :] = imag_part[:, cut]

    @pl.when(step == n // group - 1)
    def _():
        for r in range(elems):
            for q in range(chans):
                first = pl.multiple_of(scalars[slots + r * chans + q], own) * (2 * n)
                for k in range(result.shape[0]):
                    piece = result[k, pl.ds(pl.multiple_of(first, own * 2 * n), own * 2 * n), :]
                    outs[r][q, :, :, k * lanes : (k + 1) * lanes] = piece.reshape(own, 2 * n, lanes).astype(BF16)


def beamform(scalars, weights, first, n, sources, time, own, elems, chans):
    _, _, depth, beams = weights.shape
    counts = [count for _, count, _ in sources]
    group = math.gcd(math.gcd(first, n), GROUP if n >= 2 * GROUP else GROUP // 2)
    in_specs = [
        pl.BlockSpec(
            (1, group, depth // CUTS, beams), lambda i, s, part=part, j=j: (part, first // group + i, j, 0)
        )
        for part in range(2)
        for j in range(CUTS)
    ]
    for array, count, whole in sources:
        start = first if whole else 0
        in_specs.append(
            pl.BlockSpec((2 * count, group) + array.shape[2:], lambda i, s, start=start: (0, start // group + i, 0, 0))
        )
    shape = (chans, own, 2 * n, beams)
    lanes = min(128, beams)
    return pl.pallas_call(
        functools.partial(beamform_kernel, (n, group, time, own, elems, chans, counts, scalars.shape[0] - elems * chans)),
        out_shape=[jax.ShapeDtypeStruct(shape, BF16)] * elems,
        grid_spec=pltpu.PrefetchScalarGridSpec(
            num_scalar_prefetch=1,
            grid=(n // group,),
            in_specs=in_specs,
            out_specs=[pl.BlockSpec(shape, lambda i, s: (0, 0, 0, 0))] * elems,
            scratch_shapes=[
                pltpu.VMEM((group, 2 * time, depth), BF16),
                pltpu.VMEM((beams // lanes, time * 2 * n, lanes), F32),
            ],
        ),
        compiler_params=pltpu.CompilerParams(vmem_limit_bytes=VMEM_BYTES),
        cost_estimate=pl.CostEstimate(
            flops=FLOPS * n * time * depth * beams,
            bytes_accessed=4 * n * (depth * beams + time * depth + time * beams),
            transcendentals=0,
        ),
        name="beamform",
    )(scalars, *[weights] * (2 * CUTS), *[array for array, _, _ in sources])


def synthesis_kernel(layout, channels, table, *refs):
    out = refs[-1]
    times, beams = out.shape[1], out.shape[2]
    flat = out.reshape(channels * times, beams)
    lanes = min(128, beams)
    for t in range(times):
        rows, at = [], 0
        for elems, chans in layout:
            total = refs[at][0, t].astype(F32)
            for r in range(1, elems):
                total += refs[at + r][0, t].astype(F32)
            rows.append(total)
            at += elems
            for _ in range(1, chans):
                rows.append(refs[at][t].astype(F32))
                at += 1
        held = jnp.concatenate(rows, axis=0).astype(BF16)
        parts = jnp.dot(table[...], held, preferred_element_type=F32)
        half = 2 * channels
        fine = parts[:half] + (parts[half : 2 * half] + parts[2 * half :])
        out[:, t, :] = fine[:channels] * fine[:channels] + fine[channels:] * fine[channels:]


def synthesis(table, groups, channels, own, beams):
    times = 8
    in_specs = [pl.BlockSpec(table.shape, lambda i: (0, 0))]
    operands, layout = [], []
    for partials, received in groups:
        rows = partials[0].shape[2]
        layout.append((len(partials), 1 + len(received)))
        in_specs += [pl.BlockSpec((1, times, rows, beams), lambda i: (0, i, 0, 0))] * len(partials)
        in_specs += [pl.BlockSpec((times, rows, beams), lambda i: (i, 0, 0))] * len(received)
        operands += list(partials) + list(received)
    return pl.pallas_call(
        functools.partial(synthesis_kernel, layout, channels),
        out_shape=jax.ShapeDtypeStruct((channels, own, beams), F32),
        grid=(own // times,),
        in_specs=in_specs,
        out_specs=pl.BlockSpec((channels, times, beams), lambda i: (0, i, 0)),
        compiler_params=pltpu.CompilerParams(vmem_limit_bytes=VMEM_BYTES),
        cost_estimate=pl.CostEstimate(
            flops=24 * channels * channels * own * beams,
            bytes_accessed=channels * own * beams * 12,
            transcendentals=0,
        ),
        name="synthesis",
    )(table, *operands)


def synthesis_table(channels, local, plan, my_chan, chans):
    places, is_imag = [], []
    for _, first, n in plan:
        for q in range(chans):
            base = lax.rem(my_chan + chans - q, chans) * local + first
            place = base + jnp.arange(n, dtype=jnp.int32)
            places += [place, place]
            is_imag += [False] * n + [True] * n
    column = jnp.concatenate(places)
    imag = jnp.array(is_imag)
    index = jnp.arange(channels, dtype=jnp.int32)
    phase = index[:, None] * column[None, :] % channels
    angle = phase.astype(F32) * (2.0 * jnp.pi / channels)
    factor = 1.0 / jnp.sqrt(F32(channels))
    cosine, sine = jnp.cos(angle) * factor, jnp.sin(angle) * factor
    table = jnp.concatenate([jnp.where(imag, -sine, cosine), jnp.where(imag, cosine, sine)])
    high = lax.reduce_precision(table, 8, 7)
    middle = lax.reduce_precision(table - high, 8, 7)
    low = table - high - middle
    return jnp.concatenate([high, middle, low]).astype(BF16)


def after(value, other):
    return lax.optimization_barrier((value, other))[0]


def shards(voltages, weights):
    local, rows = voltages.shape[1], voltages.shape[2]
    beams = weights.shape[3]
    chans, elems, beam_devices = lax.axis_size("chan"), lax.axis_size("elem"), lax.axis_size("beam")
    channels, time = local * chans, rows * beam_devices
    own = time // (chans * elems)
    cores = 2 if beam_devices % 2 == 0 else 1
    chips = beam_devices // cores
    my_chan, my_elem, my_beam = (lax.axis_index(a) for a in ("chan", "elem", "beam"))
    my_chip, my_core = my_beam // cores, my_beam % cores

    ring = [(d, (d + cores) % beam_devices) for d in range(beam_devices)]
    pair = [(d, d ^ 1) for d in range(beam_devices)]
    plan = groups_of_channels(local)

    mate = lax.ppermute(voltages, "beam", pair) if cores == 2 else None
    table = synthesis_table(channels, local, plan, my_chan, chans)

    def offsets(core):
        return [(lax.rem(my_chip + chips - h, chips) * cores + core) * rows for h in range(chips)]

    mine, others = offsets(my_core), offsets(cores - 1 - my_core)
    piece_starts = [
        (lax.rem(my_chan + q, chans) * elems + lax.rem(my_elem + r, elems)) * own
        for r in range(elems)
        for q in range(chans)
    ]
    places = mine + (others if cores == 2 else [])
    scalars = jnp.stack(places + piece_starts).astype(jnp.int32)

    def partial_beams(k, ahead):
        gathered, first, n = plan[k]
        if gathered:
            sources = [(held[k][1], 1, False)]
        else:
            sources = [(voltages, 1, True)] + [(block, 1, False) for block in held[k][1:]]
            if cores == 2:
                sources.append((mate, 1, True))
                if k < len(plan) - 1:
                    swapped = lax.ppermute(jnp.concatenate(held[k][1:]), "beam", pair)
                    sources.append((swapped, chips - 1, False))
                else:
                    sources += [(lax.ppermute(block, "beam", pair), 1, False) for block in held[k][1:]]
        offsets_now = after(scalars, ahead) if ahead else scalars
        return beamform(offsets_now, weights, first, n, sources, time, own, elems, chans)

    def over_elements(partials):
        moved = [
            lax.ppermute(partials[r], "elem", [(d, (d + r) % elems) for d in range(elems)]) for r in range(1, elems)
        ]
        return [partials[0]] + moved

    def sums_to_send(arrived):
        totals = []
        for q in range(1, chans):
            total = arrived[0][q].astype(F32)
            for part in arrived[1:]:
                total = total + part[q].astype(F32)
            totals.append(total.astype(BF16))
        return totals

    def over_channels(totals):
        return [
            lax.ppermute(total, "chan", [(d, (d + q) % chans) for d in range(chans)])
            for q, total in enumerate(totals, 1)
        ]

    ringed = [k for k in range(len(plan)) if not plan[k][0]]
    lead = ringed[0]
    lead_piece = voltages[:, plan[lead][1] : plan[lead][1] + plan[lead][2]]
    later_pieces = after(voltages, lead_piece)
    held = [[later_pieces[:, first : first + n]] for _, first, n in plan]
    held[lead] = [lead_piece]
    for k, (gathered, _, _) in enumerate(plan):
        if gathered:
            held[k].append(lax.all_gather(held[k][0], "beam", axis=2, tiled=True))
    sent, arrived, received = [], [], []
    count = len(ringed)
    partials = []

    def work_on(k):
        ahead = []
        if k < len(plan) - UNGATED:
            if k >= Y_LAG:
                ahead += arrived[k - Y_LAG][1:]
            if k >= X_LAG:
                ahead += received[k - X_LAG]
        partials.append(partial_beams(k, ahead))
        arrived.append(over_elements(partials[k]))
        received.append(over_channels(sums_to_send(arrived[k])))

    for slot in range(count + chips + 1 + RING_LAG):
        waits = []
        if 0 <= slot - chips < count:
            work_on(slot - chips)
        if 0 <= slot - chips - RING_LAG < count:
            waits.append(partials[slot - chips - RING_LAG][-1])
        for h in range(chips - 1):
            if not 0 <= slot - h < count:
                continue
            k = ringed[slot - h]
            block = held[k][h]
            ahead = list(waits) + [sent[-w] for w in WINDOW if len(sent) >= w]
            if ahead:
                block = after(block, ahead)
            got = lax.ppermute(block, "beam", ring)
            held[k].append(got)
            sent.append(got)

    groups = [(arrived[k], received[k]) for k in range(len(plan))]
    return synthesis(table, groups, channels, own, beams)


def solution(mesh):
    placed = (P(None, "chan", "beam", "elem"), P(None, "chan", "elem", "beam"))
    return jax.shard_map(
        shards,
        mesh=mesh,
        in_specs=placed,
        out_specs=P(None, ("chan", "elem"), "beam"),
        check_vma=False,
    )
```

time: 575 us -> 369 us (0.64)
  waiting for transfers between devices: 391 us -> 259 us
  matrix products: 95.5 us -> 0 us
  Pallas kernels: 0 us -> 57.4 us
  blocking collectives: 51.7 us -> 0 us
  starting transfers between devices: 0.04 us -> 18.7 us
  between operations: 13.4 us -> 0.5 us
    all_gather x1 -> x0, waiting for transfers between devices: 293 us -> none  [shards(): volt_piece = lax.all_gather(voltages, 'beam', axis=2, tiled=True)]
    ppermute x0 -> x45, waiting for transfers between devices: none -> 259 us  [the longest x21 234 us: shards(): got = lax.ppermute(block, 'beam', ring)]
    reduce_scatter x1 -> x0, waiting for transfers between devices: 97.6 us -> none  [shards(): lax.psum_scatter(halves.astype(jnp.bfloat16), 'elem', scatter_dimension=3...]
    dot_general x8 -> x0, matrix products: 95.5 us -> none  [the longest x1 22.6 us: shards(): jnp.einsum('cte,ceb->ctb', volt_piece[1], weights[0], preferred_element_t...]
    pallas_call x0 -> x8, Pallas kernels: none -> 57.4 us  [the longest x7 51 us: beamform(): pl.pallas_call(functools.partial(beamform_kernel, (n, group, time, own, e...]
    all_to_all x1 -> x0, blocking collectives: 51.7 us -> none  [shards(): lax.all_to_all(summed, 'chan', split_axis=2, concat_axis=1, tiled=True)]
    ppermute x0 -> x45, starting transfers between devices: none -> 18.7 us  [the longest x7 8.86 us: over_channels(): lax.ppermute(total, 'chan', [(d, (d + q) % chans) for d in range(chans)])]
    unnamed x3 -> x70, local copies, waits for them, and re-layouts: 6.2 us -> 15 us
  transfers between devices with their start and end apart: 2 -> 45, of which waited for: 2 -> 23; matrix products, arithmetic and copies ran while one was open for 0% -> 4% of each run, Pallas kernels for 0% -> 13%
where the time goes in v1:
time: 369 us; the launch traced here: 368 us
  waiting for transfers between devices  259 us (70%)
  Pallas kernels  57.4 us (16%)
  local copies, waits for them, and re-layouts  20.6 us (6%)
  starting transfers between devices  18.7 us (5%)
  other arithmetic  11.4 us (3%)
    ppermute x21, waiting for transfers between devices, shards(): got = lax.ppermute(block, 'beam', ring)  234 us
    pallas_call x7, Pallas kernels, beamform(): pl.pallas_call(functools.partial(beamform_kernel, (n, group, time, own, e...  51 us
    ppermute x7, waiting for transfers between devices, over_channels(): lax.ppermute(total, 'chan', [(d, (d + q) % chans) for d in range(chans)])  15.6 us
    unnamed x70, local copies, waits for them, and re-layouts  15 us
    ppermute x7, waiting for transfers between devices, over_elements(): lax.ppermute(partials[r], 'elem', [(d, (d + r) % elems) for d in range(el...  9.46 us
    ppermute x7, starting transfers between devices, over_channels(): lax.ppermute(total, 'chan', [(d, (d + q) % chans) for d in range(chans)])  8.86 us
    concatenate x6, other arithmetic, partial_beams(): swapped = lax.ppermute(jnp.concatenate(held[k][1:]), 'beam', pair)  8.69 us
  transfers between devices with their start and end apart: 45, of which 23 were waited for; matrix products, arithmetic and copies ran while one was open for 4% of the time, Pallas kernels for 13%

profile of v1, /device:TPU:0, one launch (start us, length us, event | category | flops | bytes accessed | tf_op | source)
XLA Modules:
  0.0 368.0 jit_solution(16275602197264181063)
XLA Ops:
  4.3 19.6 %collective-permute-done.refs_5_ = bf16[2,12,16,1024]{3,2,1,0:T(8,128)(2,1)S(1)} collective-permute-done((bf16[2,12,16,1024]{3,2,1,0:T(8,128)(2,1)S(1)}, bf16[2,12,16,1024]{3,2,1,0:T(8,128)(2,1)S(1)}, u32[]{:S(2)}, u32[]{:S(2)}) %collective-permute-start) | collective-permute-done | bytes 786464 | tf_op jit(solution)/shard_map/ppermute | solution.py:299
  23.9 20.5 %collective-permute-done.1.refs_6_ = bf16[2,12,16,1024]{3,2,1,0:T(8,128)(2,1)S(1)} collective-permute-done((bf16[2,12,16,1024]{3,2,1,0:T(8,128)(2,1)S(1)}, bf16[2,12,16,1024]{3,2,1,0:T(8,128)(2,1)S(1)}, u32[]{:S(2)}, u32[]{:S(2)}) %collective-permute-start.1) | collective-permute-done | bytes 786464 | tf_op jit(solution)/shard_map/ppermute | solution.py:299
  47.8 18.9 %collective-permute-done.2.refs_7_ = bf16[2,12,16,1024]{3,2,1,0:T(8,128)(2,1)S(1)} collective-permute-done((bf16[2,12,16,1024]{3,2,1,0:T(8,128)(2,1)S(1)}, bf16[2,12,16,1024]{3,2,1,0:T(8,128)(2,1)S(1)}, u32[]{:S(2)}, u32[]{:S(2)}) %collective-permute-start.2) | collective-permute-done | bytes 786464 | tf_op jit(solution)/shard_map/ppermute | solution.py:299
  68.3 12.5 %collective-permute-done.7.refs_5_ = bf16[2,12,16,1024]{3,2,1,0:T(8,128)(2,1)S(1)} collective-permute-done((bf16[2,12,16,1024]{3,2,1,0:T(8,128)(2,1)S(1)}, bf16[2,12,16,1024]{3,2,1,0:T(8,128)(2,1)S(1)}, u32[]{:S(2)}, u32[]{:S(2)}) %collective-permute-start.7) | collective-permute-done | bytes 786464 | tf_op jit(solution)/shard_map/ppermute | solution.py:299
  80.8 18.7 %collective-permute-done.8.refs_6_ = bf16[2,12,16,1024]{3,2,1,0:T(8,128)(2,1)S(1)} collective-permute-done((bf16[2,12,16,1024]{3,2,1,0:T(8,128)(2,1)S(1)}, bf16[2,12,16,1024]{3,2,1,0:T(8,128)(2,1)S(1)}, u32[]{:S(2)}, u32[]{:S(2)}) %collective-permute-start.8) | collective-permute-done | bytes 786464 | tf_op jit(solution)/shard_map/ppermute | solution.py:299
  99.5 22.3 %collective-permute-done.9.refs_7_ = bf16[2,12,16,1024]{3,2,1,0:T(8,128)(2,1)S(1)} collective-permute-done((bf16[2,12,16,1024]{3,2,1,0:T(8,128)(2,1)S(1)}, bf16[2,12,16,1024]{3,2,1,0:T(8,128)(2,1)S(1)}, u32[]{:S(2)}, u32[]{:S(2)}) %collective-permute-start.9) | collective-permute-done | bytes 786464 | tf_op jit(solution)/shard_map/ppermute | solution.py:299
  123.6 10.5 %collective-permute-done.13.refs_5_ = bf16[2,12,16,1024]{3,2,1,0:T(8,128)(2,1)S(1)} collective-permute-done((bf16[2,12,16,1024]{3,2,1,0:T(8,128)(2,1)}, bf16[2,12,16,1024]{3,2,1,0:T(8,128)(2,1)S(1)}, u32[]{:S(2)}, u32[]{:S(2)}) %collective-permute-start.13) | collective-permute-done | bytes 786464 | tf_op jit(solution)/shard_map/ppermute | solution.py:299
  138.6 8.6 %beamform.7 = (bf16[2,32,24,256]{3,2,1,0:T(8,128)(2,1)S(1)}, bf16[2,32,24,256]{3,2,1,0:T(8,128)(2,1)S(1)}) custom-call(s32[12]{0:T(128)S(1)} %stack.51.scalars, bf16[2,64,1024,256]{3,2,1,0:T(8,128)(2,1)} %refs_3_.13, bf16[2,64,1024,256]{3,2,1,0:T(8,128)(2,1)} %refs_3_.13, bf16[2,64,1024,256]{3,2,1,0:T(8,128)(2,1)} %refs_3_.13, ...), custom_call_target="tpu_custom_call" | custom-call | flops 12884901888 | bytes 20447232 | tf_op jit(solution)/shard_map/beamform/pallas_call | solution.py:96
  147.9 21.0 %collective-permute-done.14.refs_6_ = bf16[2,12,16,1024]{3,2,1,0:T(8,128)(2,1)S(1)} collective-permute-done((bf16[2,12,16,1024]{3,2,1,0:T(8,128)(2,1)S(1)}, bf16[2,12,16,1024]{3,2,1,0:T(8,128)(2,1)S(1)}, u32[]{:S(2)}, u32[]{:S(2)}) %collective-permute-start.14) | collective-permute-done | bytes 786464 | tf_op jit(solution)/shard_map/ppermute | solution.py:299
  168.9 22.2 %collective-permute-done.15.refs_7_ = bf16[2,12,16,1024]{3,2,1,0:T(8,128)(2,1)S(1)} collective-permute-done((bf16[2,12,16,1024]{3,2,1,0:T(8,128)(2,1)S(1)}, bf16[2,12,16,1024]{3,2,1,0:T(8,128)(2,1)S(1)}, u32[]{:S(2)}, u32[]{:S(2)}) %collective-permute-start.15) | collective-permute-done | bytes 786464 | tf_op jit(solution)/shard_map/ppermute | solution.py:299
  192.9 8.7 %beamform.8 = (bf16[2,32,24,256]{3,2,1,0:T(8,128)(2,1)S(1)}, bf16[2,32,24,256]{3,2,1,0:T(8,128)(2,1)S(1)}) custom-call(s32[12]{0:T(128)S(1)} %stack.51.scalars, bf16[2,64,1024,256]{3,2,1,0:T(8,128)(2,1)} %refs_3_.13, bf16[2,64,1024,256]{3,2,1,0:T(8,128)(2,1)} %refs_3_.13, bf16[2,64,1024,256]{3,2,1,0:T(8,128)(2,1)} %refs_3_.13, ...), custom_call_target="tpu_custom_call" | custom-call | flops 12884901888 | bytes 20447232 | tf_op jit(solution)/shard_map/beamform/pallas_call | solution.py:96
  204.0 19.9 %collective-permute-done.21.refs_7_ = bf16[2,12,16,1024]{3,2,1,0:T(8,128)(2,1)S(1)} collective-permute-done((bf16[2,12,16,1024]{3,2,1,0:T(8,128)(2,1)S(1)}, bf16[2,12,16,1024]{3,2,1,0:T(8,128)(2,1)S(1)}, u32[]{:S(2)}, u32[]{:S(2)}) %collective-permute-start.21) | collective-permute-done | bytes 786464 | tf_op jit(solution)/shard_map/ppermute | solution.py:299
  224.2 10.3 %collective-permute-done.25.refs_5_ = bf16[2,8,16,1024]{3,2,1,0:T(8,128)(2,1)S(1)} collective-permute-done((bf16[2,8,16,1024]{3,2,1,0:T(8,128)(2,1)S(1)}, bf16[2,8,16,1024]{3,2,1,0:T(8,128)(2,1)S(1)}, u32[]{:S(2)}, u32[]{:S(2)}) %collective-permute-start.25) | collective-permute-done | bytes 524320 | tf_op jit(solution)/shard_map/ppermute | solution.py:299
  235.3 8.1 %beamform.9 = (bf16[2,32,24,256]{3,2,1,0:T(8,128)(2,1)S(1)}, bf16[2,32,24,256]{3,2,1,0:T(8,128)(2,1)S(1)}) custom-call(s32[12]{0:T(128)S(1)} %stack.51.scalars, bf16[2,64,1024,256]{3,2,1,0:T(8,128)(2,1)} %refs_3_.13, bf16[2,64,1024,256]{3,2,1,0:T(8,128)(2,1)} %refs_3_.13, bf16[2,64,1024,256]{3,2,1,0:T(8,128)(2,1)} %refs_3_.13, ...), custom_call_target="tpu_custom_call" | custom-call | flops 12884901888 | bytes 20447232 | tf_op jit(solution)/shard_map/beamform/pallas_call | solution.py:96
  244.1 5.7 %collective-permute-done.26.refs_6_ = bf16[2,8,16,1024]{3,2,1,0:T(8,128)(2,1)S(1)} collective-permute-done((bf16[2,8,16,1024]{3,2,1,0:T(8,128)(2,1)S(1)}, bf16[2,8,16,1024]{3,2,1,0:T(8,128)(2,1)S(1)}, u32[]{:S(2)}, u32[]{:S(2)}) %collective-permute-start.26) | collective-permute-done | bytes 524320 | tf_op jit(solution)/shard_map/ppermute | solution.py:299
  251.4 18.3 %collective-permute-done.31.refs_5_ = bf16[2,4,16,1024]{3,2,1,0:T(8,128)(2,1)S(1)} collective-permute-done((bf16[2,4,16,1024]{3,2,1,0:T(8,128)(2,1)S(1)}, bf16[2,4,16,1024]{3,2,1,0:T(8,128)(2,1)S(1)}, u32[]{:S(2)}, u32[]{:S(2)}) %collective-permute-start.31) | collective-permute-done | bytes 262176 | tf_op jit(solution)/shard_map/ppermute | solution.py:299
  271.0 9.0 %beamform.10 = (bf16[2,32,24,256]{3,2,1,0:T(8,128)(2,1)S(1)}, bf16[2,32,24,256]{3,2,1,0:T(8,128)(2,1)}) custom-call(s32[12]{0:T(128)S(1)} %stack.51.scalars, bf16[2,64,1024,256]{3,2,1,0:T(8,128)(2,1)} %refs_3_.13, bf16[2,64,1024,256]{3,2,1,0:T(8,128)(2,1)} %refs_3_.13, bf16[2,64,1024,256]{3,2,1,0:T(8,128)(2,1)} %refs_3_.13, ...), custom_call_target="tpu_custom_call" | custom-call | flops 12884901888 | bytes 20447232 | tf_op jit(solution)/shard_map/beamform/pallas_call | solution.py:96
  283.9 8.2 %collective-permute-done.37.refs_5_ = bf16[2,4,16,1024]{3,2,1,0:T(8,128)(2,1)} collective-permute-done((bf16[2,4,16,1024]{3,2,1,0:T(8,128)(2,1)}, bf16[2,4,16,1024]{3,2,1,0:T(8,128)(2,1)}, u32[]{:S(2)}, u32[]{:S(2)}) %collective-permute-start.37) | collective-permute-done | bytes 262176 | tf_op jit(solution)/shard_map/ppermute | solution.py:299
  292.1 5.6 %collective-permute-done.33.refs_7_ = bf16[2,4,16,1024]{3,2,1,0:T(8,128)(2,1)} collective-permute-done((bf16[2,4,16,1024]{3,2,1,0:T(8,128)(2,1)}, bf16[2,4,16,1024]{3,2,1,0:T(8,128)(2,1)}, u32[]{:S(2)}, u32[]{:S(2)}) %collective-permute-start.33) | collective-permute-done | bytes 262176 | tf_op jit(solution)/shard_map/ppermute | solution.py:299
  302.4 7.3 %beamform.11 = (bf16[2,32,16,256]{3,2,1,0:T(8,128)(2,1)S(1)}, bf16[2,32,16,256]{3,2,1,0:T(8,128)(2,1)}) custom-call(s32[12]{0:T(128)S(1)} %stack.51.scalars, bf16[2,64,1024,256]{3,2,1,0:T(8,128)(2,1)} %refs_3_.13, bf16[2,64,1024,256]{3,2,1,0:T(8,128)(2,1)} %refs_3_.13, bf16[2,64,1024,256]{3,2,1,0:T(8,128)(2,1)} %refs_3_.13, ...), custom_call_target="tpu_custom_call" | custom-call | flops 8589934592 | bytes 13631488 | tf_op jit(solution)/shard_map/beamform/pallas_call | solution.py:96
  313.1 9.6 %collective-permute-done.24.refs_11_ = bf16[32,24,256]{2,1,0:T(8,128)(2,1)S(1)} collective-permute-done((bf16[32,24,256]{2,1,0:T(8,128)(2,1)S(1)}, bf16[32,24,256]{2,1,0:T(8,128)(2,1)S(1)}, u32[]{:S(2)}, u32[]{:S(2)}) %collective-permute-start.24) | collective-permute-done | bytes 393248 | tf_op jit(solution)/shard_map/ppermute | solution.py:257
  327.8 4.8 %beamform.12 = (bf16[2,32,8,256]{3,2,1,0:T(8,128)(2,1)S(1)}, bf16[2,32,8,256]{3,2,1,0:T(8,128)(2,1)}) custom-call(s32[12]{0:T(128)S(1)} %stack.51.scalars, bf16[2,64,1024,256]{3,2,1,0:T(8,128)(2,1)} %refs_3_.13, bf16[2,64,1024,256]{3,2,1,0:T(8,128)(2,1)} %refs_3_.13, bf16[2,64,1024,256]{3,2,1,0:T(8,128)(2,1)} %refs_3_.13, ...), custom_call_target="tpu_custom_call" | custom-call | flops 4294967296 | bytes 6815744 | tf_op jit(solution)/shard_map/beamform/pallas_call | solution.py:96
  335.6 4.8 %collective-permute-done.35.refs_16_ = bf16[2,32,8,256]{3,2,1,0:T(8,128)(2,1)S(1)} collective-permute-done((bf16[2,32,8,256]{3,2,1,0:T(8,128)(2,1)}, bf16[2,32,8,256]{3,2,1,0:T(8,128)(2,1)S(1)}, u32[]{:S(2)}, u32[]{:S(2)}) %collective-permute-start.35) | collective-permute-done | bytes 262176 | tf_op jit(solution)/shard_map/ppermute | solution.py:242
  361.7 6.3 %synthesis.1 = f32[128,32,256]{2,1,0:T(8,128)} custom-call(bf16[768,256]{1,0:T(8,128)(2,1)S(1)} %pad_maximum_fusion.6.table, bf16[2,32,24,256]{3,2,1,0:T(8,128)(2,1)S(1)} %copy-done.11, bf16[2,32,24,256]{3,2,1,0:T(8,128)(2,1)S(1)} %copy-done.13, bf16[32,24,256]{2,1,0:T(8,128)(2,1)S(1)} %copy-done.27, bf16[2,32,24,256]{3,2,1,0:T(8,128)(2,1)S(1)} %copy-done.15, ...), custom_call_target="tpu_custom_call" | custom-call | flops 3221225472 | bytes 12582912 | tf_op jit(solution)/shard_map/synthesis/pallas_call | solution.py:152
  (173 shorter events, 66.1 us)
Async XLA Ops:
  1.2 22.6 %collective-permute-start = (bf16[2,12,16,1024]{3,2,1,0:T(8,128)(2,1)S(1)}, bf16[2,12,16,1024]{3,2,1,0:T(8,128)(2,1)S(1)}, u32[]{:S(2)}, u32[]{:S(2)}) collective-permute-start(bf16[2,12,16,1024]{3,2,1,0:T(8,128)(2,1)S(1)} %slice.63), channel_id=1, source_target_pairs={{0,2},{1,3},{2,4},{3,5},{4,6},{5,7},{6,0},{7,1},{8,10},{9,11},{10,... | collective-permute-start | bytes 2359304 | tf_op jit(solution)/shard_map/ppermute | solution.py:299
  4.3 129.9 %collective-permute-start.3 = (bf16[2,64,16,1024]{3,2,1,0:T(8,128)(2,1)}, bf16[2,64,16,1024]{3,2,1,0:T(8,128)(2,1)}, u32[]{:S(2)}, u32[]{:S(2)}) collective-permute-start(bf16[2,64,16,1024]{3,2,1,0:T(8,128)(2,1)} %refs_4_.13), channel_id=1, source_target_pairs={{0,1},{1,0},{2,3},{3,2},{4,5},{5,4},{6,7},{7,6},{8,9},{9,8},{10,11... | collective-permute-start | bytes 12582920 | tf_op jit(solution)/shard_map/ppermute | solution.py:209
  44.4 22.3 %collective-permute-start.2 = (bf16[2,12,16,1024]{3,2,1,0:T(8,128)(2,1)S(1)}, bf16[2,12,16,1024]{3,2,1,0:T(8,128)(2,1)S(1)}, u32[]{:S(2)}, u32[]{:S(2)}) collective-permute-start(bf16[2,12,16,1024]{3,2,1,0:T(8,128)(2,1)S(1)} %collective-permute-done.1.refs_6_), channel_id=1, source_target_pairs={{0,2},{1,3},{2,4},{3,5},{4,6},{5,7},{6,0},{7,1},{8,10},{9,11},{10,... | collective-permute-start | bytes 2359304 | tf_op jit(solution)/shard_map/ppermute | solution.py:299
  47.8 33.0 %collective-permute-start.7 = (bf16[2,12,16,1024]{3,2,1,0:T(8,128)(2,1)S(1)}, bf16[2,12,16,1024]{3,2,1,0:T(8,128)(2,1)S(1)}, u32[]{:S(2)}, u32[]{:S(2)}) collective-permute-start(bf16[2,12,16,1024]{3,2,1,0:T(8,128)(2,1)S(1)} %get-tuple-element.87), channel_id=1, source_target_pairs={{0,2},{1,3},{2,4},{3,5},{4,6},{5,7},{6,0},{7,1},{8,10},{9,11},{10,... | collective-permute-start | bytes 2359304 | tf_op jit(solution)/shard_map/ppermute | solution.py:299
  68.3 65.8 %collective-permute-start.4 = (bf16[6,12,16,1024]{3,2,1,0:T(8,128)(2,1)}, bf16[6,12,16,1024]{3,2,1,0:T(8,128)(2,1)}, u32[]{:S(2)}, u32[]{:S(2)}) collective-permute-start(bf16[6,12,16,1024]{3,2,1,0:T(8,128)(2,1)} %pad_maximum_fusion), channel_id=1, source_target_pairs={{0,1},{1,0},{2,3},{3,2},{4,5},{5,4},{6,7},{7,6},{8,9},{9,8},{10,11... | collective-permute-start | bytes 7077896 | tf_op jit(solution)/shard_map/ppermute | solution.py:233
  99.5 22.3 %collective-permute-start.9 = (bf16[2,12,16,1024]{3,2,1,0:T(8,128)(2,1)S(1)}, bf16[2,12,16,1024]{3,2,1,0:T(8,128)(2,1)S(1)}, u32[]{:S(2)}, u32[]{:S(2)}) collective-permute-start(bf16[2,12,16,1024]{3,2,1,0:T(8,128)(2,1)S(1)} %collective-permute-done.8.refs_6_), channel_id=1, source_target_pairs={{0,2},{1,3},{2,4},{3,5},{4,6},{5,7},{6,0},{7,1},{8,10},{9,11},{10,... | collective-permute-start | bytes 2359304 | tf_op jit(solution)/shard_map/ppermute | solution.py:299
  99.5 34.6 %collective-permute-start.13 = (bf16[2,12,16,1024]{3,2,1,0:T(8,128)(2,1)}, bf16[2,12,16,1024]{3,2,1,0:T(8,128)(2,1)S(1)}, u32[]{:S(2)}, u32[]{:S(2)}) collective-permute-start(bf16[2,12,16,1024]{3,2,1,0:T(8,128)(2,1)} %get-tuple-element.54), channel_id=1, source_target_pairs={{0,2},{1,3},{2,4},{3,5},{4,6},{5,7},{6,0},{7,1},{8,10},{9,11},{10,... | collective-permute-start | bytes 2359304 | tf_op jit(solution)/shard_map/ppermute | solution.py:299
  123.5 69.3 %collective-permute-start.10 = (bf16[6,12,16,1024]{3,2,1,0:T(8,128)(2,1)}, bf16[6,12,16,1024]{3,2,1,0:T(8,128)(2,1)}, u32[]{:S(2)}, u32[]{:S(2)}) collective-permute-start(bf16[6,12,16,1024]{3,2,1,0:T(8,128)(2,1)} %pad_maximum_fusion.1), channel_id=1, source_target_pairs={{0,1},{1,0},{2,3},{3,2},{4,5},{5,4},{6,7},{7,6},{8,9},{9,8},{10,11... | collective-permute-start | bytes 7077896 | tf_op jit(solution)/shard_map/ppermute | solution.py:233
  134.1 34.8 %collective-permute-start.19 = (bf16[2,12,16,1024]{3,2,1,0:T(8,128)(2,1)}, bf16[2,12,16,1024]{3,2,1,0:T(8,128)(2,1)S(1)}, u32[]{:S(2)}, u32[]{:S(2)}) collective-permute-start(bf16[2,12,16,1024]{3,2,1,0:T(8,128)(2,1)} %get-tuple-element.60), channel_id=1, source_target_pairs={{0,2},{1,3},{2,4},{3,5},{4,6},{5,7},{6,0},{7,1},{8,10},{9,11},{10,... | collective-permute-start | bytes 2359304 | tf_op jit(solution)/shard_map/ppermute | solution.py:299
  134.1 34.8 %collective-permute-start.14 = (bf16[2,12,16,1024]{3,2,1,0:T(8,128)(2,1)S(1)}, bf16[2,12,16,1024]{3,2,1,0:T(8,128)(2,1)S(1)}, u32[]{:S(2)}, u32[]{:S(2)}) collective-permute-start(bf16[2,12,16,1024]{3,2,1,0:T(8,128)(2,1)S(1)} %collective-permute-done.13.refs_5_), channel_id=1, source_target_pairs={{0,2},{1,3},{2,4},{3,5},{4,6},{5,7},{6,0},{7,1},{8,10},{9,11},{10,... | collective-permute-start | bytes 2359304 | tf_op jit(solution)/shard_map/ppermute | solution.py:299
  147.3 21.6 %collective-permute-start.5 = (bf16[2,32,24,256]{3,2,1,0:T(8,128)(2,1)S(1)}, bf16[2,32,24,256]{3,2,1,0:T(8,128)(2,1)S(1)}, u32[]{:S(2)}, u32[]{:S(2)}) collective-permute-start(bf16[2,32,24,256]{3,2,1,0:T(8,128)(2,1)S(1)} %get-tuple-element.46), channel_id=1, source_target_pairs={{0,8},{8,0},{1,9},{9,1},{2,10},{10,2},{3,11},{11,3},{4,12},{12,4},... | collective-permute-start | bytes 2359304 | tf_op jit(solution)/shard_map/ppermute | solution.py:242
  168.9 22.3 %collective-permute-start.15 = (bf16[2,12,16,1024]{3,2,1,0:T(8,128)(2,1)S(1)}, bf16[2,12,16,1024]{3,2,1,0:T(8,128)(2,1)S(1)}, u32[]{:S(2)}, u32[]{:S(2)}) collective-permute-start(bf16[2,12,16,1024]{3,2,1,0:T(8,128)(2,1)S(1)} %collective-permute-done.14.refs_6_), channel_id=1, source_target_pairs={{0,2},{1,3},{2,4},{3,5},{4,6},{5,7},{6,0},{7,1},{8,10},{9,11},{10,... | collective-permute-start | bytes 2359304 | tf_op jit(solution)/shard_map/ppermute | solution.py:299
  168.9 32.8 %collective-permute-start.20 = (bf16[2,12,16,1024]{3,2,1,0:T(8,128)(2,1)S(1)}, bf16[2,12,16,1024]{3,2,1,0:T(8,128)(2,1)S(1)}, u32[]{:S(2)}, u32[]{:S(2)}) collective-permute-start(bf16[2,12,16,1024]{3,2,1,0:T(8,128)(2,1)S(1)} %collective-permute-done.19.refs_5_), channel_id=1, source_target_pairs={{0,2},{1,3},{2,4},{3,5},{4,6},{5,7},{6,0},{7,1},{8,10},{9,11},{10,... | collective-permute-start | bytes 2359304 | tf_op jit(solution)/shard_map/ppermute | solution.py:299
  192.8 42.5 %collective-permute-start.16 = (bf16[6,12,16,1024]{3,2,1,0:T(8,128)(2,1)}, bf16[6,12,16,1024]{3,2,1,0:T(8,128)(2,1)S(1)}, u32[]{:S(2)}, u32[]{:S(2)}) collective-permute-start(bf16[6,12,16,1024]{3,2,1,0:T(8,128)(2,1)} %pad_maximum_fusion.2), channel_id=1, source_target_pairs={{0,1},{1,0},{2,3},{3,2},{4,5},{5,4},{6,7},{7,6},{8,9},{9,8},{10,11... | collective-permute-start | bytes 7077896 | tf_op jit(solution)/shard_map/ppermute | solution.py:233
  201.7 22.2 %collective-permute-start.21 = (bf16[2,12,16,1024]{3,2,1,0:T(8,128)(2,1)S(1)}, bf16[2,12,16,1024]{3,2,1,0:T(8,128)(2,1)S(1)}, u32[]{:S(2)}, u32[]{:S(2)}) collective-permute-start(bf16[2,12,16,1024]{3,2,1,0:T(8,128)(2,1)S(1)} %collective-permute-done.20.refs_6_), channel_id=1, source_target_pairs={{0,2},{1,3},{2,4},{3,5},{4,6},{5,7},{6,0},{7,1},{8,10},{9,11},{10,... | collective-permute-start | bytes 2359304 | tf_op jit(solution)/shard_map/ppermute | solution.py:299
  201.7 33.6 %collective-permute-start.11 = (bf16[2,32,24,256]{3,2,1,0:T(8,128)(2,1)S(1)}, bf16[2,32,24,256]{3,2,1,0:T(8,128)(2,1)S(1)}, u32[]{:S(2)}, u32[]{:S(2)}) collective-permute-start(bf16[2,32,24,256]{3,2,1,0:T(8,128)(2,1)S(1)} %get-tuple-element.52), channel_id=1, source_target_pairs={{0,8},{8,0},{1,9},{9,1},{2,10},{10,2},{3,11},{11,3},{4,12},{12,4},... | collective-permute-start | bytes 2359304 | tf_op jit(solution)/shard_map/ppermute | solution.py:242
  202.3 32.3 %collective-permute-start.25 = (bf16[2,8,16,1024]{3,2,1,0:T(8,128)(2,1)S(1)}, bf16[2,8,16,1024]{3,2,1,0:T(8,128)(2,1)S(1)}, u32[]{:S(2)}, u32[]{:S(2)}) collective-permute-start(bf16[2,8,16,1024]{3,2,1,0:T(8,128)(2,1)S(1)} %slice.75), channel_id=1, source_target_pairs={{0,2},{1,3},{2,4},{3,5},{4,6},{5,7},{6,0},{7,1},{8,10},{9,11},{10,... | collective-permute-start | bytes 1572872 | tf_op jit(solution)/shard_map/ppermute | solution.py:299
  202.5 32.1 %collective-permute-start.6 = (bf16[32,24,256]{2,1,0:T(8,128)(2,1)S(1)}, bf16[32,24,256]{2,1,0:T(8,128)(2,1)S(1)}, u32[]{:S(2)}, u32[]{:S(2)}) collective-permute-start(bf16[32,24,256]{2,1,0:T(8,128)(2,1)S(1)} %fusion), channel_id=1, source_target_pairs={{0,16},{16,0},{1,17},{17,1},{2,18},{18,2},{3,19},{19,3},{4,20},{20... | collective-permute-start | bytes 1179656 | tf_op jit(solution)/shard_map/ppermute | solution.py:257
  224.2 46.8 %collective-permute-start.22 = (bf16[6,12,16,1024]{3,2,1,0:T(8,128)(2,1)S(1)}, bf16[6,12,16,1024]{3,2,1,0:T(8,128)(2,1)S(1)}, u32[]{:S(2)}, u32[]{:S(2)}) collective-permute-start(bf16[6,12,16,1024]{3,2,1,0:T(8,128)(2,1)S(1)} %pad_maximum_fusion.3), channel_id=1, source_target_pairs={{0,1},{1,0},{2,3},{3,2},{4,5},{5,4},{6,7},{7,6},{8,9},{9,8},{10,11... | collective-permute-start | bytes 7077896 | tf_op jit(solution)/shard_map/ppermute | solution.py:233
  243.5 27.5 %collective-permute-start.17 = (bf16[2,32,24,256]{3,2,1,0:T(8,128)(2,1)S(1)}, bf16[2,32,24,256]{3,2,1,0:T(8,128)(2,1)S(1)}, u32[]{:S(2)}, u32[]{:S(2)}) collective-permute-start(bf16[2,32,24,256]{3,2,1,0:T(8,128)(2,1)S(1)} %get-tuple-element.58), channel_id=1, source_target_pairs={{0,8},{8,0},{1,9},{9,1},{2,10},{10,2},{3,11},{11,3},{4,12},{12,4},... | collective-permute-start | bytes 2359304 | tf_op jit(solution)/shard_map/ppermute | solution.py:242
  271.0 29.2 %collective-permute-start.28 = (bf16[6,8,16,1024]{3,2,1,0:T(8,128)(2,1)}, bf16[6,8,16,1024]{3,2,1,0:T(8,128)(2,1)}, u32[]{:S(2)}, u32[]{:S(2)}) collective-permute-start(bf16[6,8,16,1024]{3,2,1,0:T(8,128)(2,1)} %pad_maximum_fusion.4), channel_id=1, source_target_pairs={{0,1},{1,0},{2,3},{3,2},{4,5},{5,4},{6,7},{7,6},{8,9},{9,8},{10,11... | collective-permute-start | bytes 4718600 | tf_op jit(solution)/shard_map/ppermute | solution.py:233
  292.1 20.9 %collective-permute-start.38 = (bf16[2,4,16,1024]{3,2,1,0:T(8,128)(2,1)}, bf16[2,4,16,1024]{3,2,1,0:T(8,128)(2,1)}, u32[]{:S(2)}, u32[]{:S(2)}) collective-permute-start(bf16[2,4,16,1024]{3,2,1,0:T(8,128)(2,1)} %collective-permute-done.37.refs_5_), channel_id=1, source_target_pairs={{0,2},{1,3},{2,4},{3,5},{4,6},{5,7},{6,0},{7,1},{8,10},{9,11},{10,... | collective-permute-start | bytes 786440 | tf_op jit(solution)/shard_map/ppermute | solution.py:299
  299.8 24.9 %collective-permute-start.34 = (bf16[6,4,16,1024]{3,2,1,0:T(8,128)(2,1)}, bf16[6,4,16,1024]{3,2,1,0:T(8,128)(2,1)}, u32[]{:S(2)}, u32[]{:S(2)}) collective-permute-start(bf16[6,4,16,1024]{3,2,1,0:T(8,128)(2,1)} %pad_maximum_fusion.5), channel_id=1, source_target_pairs={{0,1},{1,0},{2,3},{3,2},{4,5},{5,4},{6,7},{7,6},{8,9},{9,8},{10,11... | collective-permute-start | bytes 2359304 | tf_op jit(solution)/shard_map/ppermute | solution.py:233
  313.1 30.0 %collective-permute-start.40 = (bf16[2,4,16,1024]{3,2,1,0:T(8,128)(2,1)}, bf16[2,4,16,1024]{3,2,1,0:T(8,128)(2,1)}, u32[]{:S(2)}, u32[]{:S(2)}) collective-permute-start(bf16[2,4,16,1024]{3,2,1,0:T(8,128)(2,1)} %collective-permute-done.37.refs_5_), channel_id=1, source_target_pairs={{0,1},{1,0},{2,3},{3,2},{4,5},{5,4},{6,7},{7,6},{8,9},{9,8},{10,11... | collective-permute-start | bytes 786440 | tf_op jit(solution)/shard_map/ppermute | solution.py:236
  (56 other events, 826.3 us)

commit v2 on v1

--- a/solution.py
+++ b/solution.py
@@ -11,12 +11,15 @@
 F32 = jnp.float32
 BF16 = jnp.bfloat16
 VMEM_BYTES = 40 * 2**20
-WINDOW = (3,)
-Y_LAG, X_LAG, RING_LAG, UNGATED = 1, 2, 0, 0
-FLOPS = 32
+WINDOW = (2,)
+Y_LAG, X_LAG, RING_LAG, UNGATED = 2, 3, 0, 1
+FLOPS = 0
+TAIL_GATE = 3
+TABLE_SLOT = 1
+SKEW, SPLIT_SWAPS = 1, 1
 CUTS = 2
 GROUP = 4
-PLAN = ((0, 6), (0, 6), (0, 6), (0, 6), (0, 4), (0, 2), (0, 2))
+PLAN = ((0, 4), (0, 4), (0, 4), (0, 4), (0, 4), (0, 4), (0, 4), (0, 2), (0, 2))
 
 
 def groups_of_channels(channels):
@@ -109,7 +112,7 @@
         compiler_params=pltpu.CompilerParams(vmem_limit_bytes=VMEM_BYTES),
         cost_estimate=pl.CostEstimate(
             flops=FLOPS * n * time * depth * beams,
-            bytes_accessed=4 * n * (depth * beams + time * depth + time * beams),
+            bytes_accessed=FLOPS * n * (depth * beams + time * depth + time * beams) // 8,
             transcendentals=0,
         ),
         name="beamform",
@@ -229,11 +232,14 @@
             sources = [(voltages, 1, True)] + [(block, 1, False) for block in held[k][1:]]
             if cores == 2:
                 sources.append((mate, 1, True))
-                if k < len(plan) - 1:
-                    swapped = lax.ppermute(jnp.concatenate(held[k][1:]), "beam", pair)
-                    sources.append((swapped, chips - 1, False))
-                else:
-                    sources += [(lax.ppermute(block, "beam", pair), 1, False) for block in held[k][1:]]
+                blocks = held[k][1:]
+            if k >= 1 and k >= len(plan) - TAIL_GATE:
+                blocks = blocks[:-1] + [after(blocks[-1], partials[k - 1][-1])]
+            if k < len(plan) - SPLIT_SWAPS:
+                early = blocks[:-1]
+                sources.append((lax.ppermute(jnp.concatenate(early), "beam", pair), len(early), False))
+                blocks = blocks[-1:]
+            sources += [(lax.ppermute(block, "beam", pair), 1, False) for block in blocks]
         offsets_now = after(scalars, ahead) if ahead else scalars
         return beamform(offsets_now, weights, first, n, sources, time, own, elems, chans)
 
@@ -282,22 +288,25 @@
         arrived.append(over_elements(partials[k]))
         received.append(over_channels(sums_to_send(arrived[k])))
 
-    for slot in range(count + chips + 1 + RING_LAG):
+    depth = SKEW * (chips - 2) + 1
+    for slot in range(count + depth + RING_LAG + 1):
         waits = []
-        if 0 <= slot - chips < count:
-            work_on(slot - chips)
-        if 0 <= slot - chips - RING_LAG < count:
-            waits.append(partials[slot - chips - RING_LAG][-1])
+        if 0 <= slot - depth - 1 < count:
+            work_on(slot - depth - 1)
+        if 0 <= slot - depth - 1 - RING_LAG < count:
+            waits.append(partials[slot - depth - 1 - RING_LAG][-1])
+        if slot == TABLE_SLOT:
+            waits.append(table)
         for h in range(chips - 1):
-            if not 0 <= slot - h < count:
+            k = slot - SKEW * h
+            if not 0 <= k < count:
                 continue
-            k = ringed[slot - h]
-            block = held[k][h]
+            block = held[ringed[k]][h]
             ahead = list(waits) + [sent[-w] for w in WINDOW if len(sent) >= w]
             if ahead:
                 block = after(block, ahead)
             got = lax.ppermute(block, "beam", ring)
-            held[k].append(got)
+            held[ringed[k]].append(got)
             sent.append(got)
 
     groups = [(arrived[k], received[k]) for k in range(len(plan))]

time: 369 us -> 328 us (0.89)
  waiting for transfers between devices: 259 us -> 212 us
  starting transfers between devices: 18.7 us -> 36.1 us
  local copies, waits for them, and re-layouts: 20.6 us -> 13.5 us
  other arithmetic: 11.4 us -> 6.51 us
    ppermute x21 -> x27, waiting for transfers between devices: 234 us -> 192 us  [shards(): got = lax.ppermute(block, 'beam', ring)]
    ppermute x7 -> x9, starting transfers between devices: 5.35 us -> 12.7 us  [over_elements(): lax.ppermute(partials[r], 'elem', [(d, (d + r) % elems) for d in range(el...]
    unnamed x70 -> x50, local copies, waits for them, and re-layouts: 15 us -> 8.27 us
    concatenate x6 -> x8, other arithmetic: 8.69 us -> 3.61 us  [partial_beams(): jnp.concatenate(early)]
    ppermute x21 -> x27, starting transfers between devices: 3.85 us -> 8.85 us  [shards(): got = lax.ppermute(block, 'beam', ring)]
    ppermute x7 -> x9, starting transfers between devices: 8.86 us -> 12.9 us  [over_channels(): lax.ppermute(total, 'chan', [(d, (d + q) % chans) for d in range(chans)])]
    ppermute x7 -> x9, waiting for transfers between devices: 9.46 us -> 6.73 us  [over_elements(): lax.ppermute(partials[r], 'elem', [(d, (d + r) % elems) for d in range(el...]
    ppermute x7 -> x9, waiting for transfers between devices: 15.6 us -> 13.7 us  [over_channels(): lax.ppermute(total, 'chan', [(d, (d + q) % chans) for d in range(chans)])]
  transfers between devices with their start and end apart: 45 -> 65, of which waited for: 23 -> 32; matrix products, arithmetic and copies ran while one was open for 4% -> 4% of each run, Pallas kernels for 13% -> 16%
where the time goes in v2:
time: 328 us
  waiting for transfers between devices  212 us (65%)
  Pallas kernels  59.2 us (18%)
  starting transfers between devices  36.1 us (11%)
  local copies, waits for them, and re-layouts  13.5 us (4%)
  other arithmetic  6.51 us (2%)
    ppermute x27, waiting for transfers between devices, shards(): got = lax.ppermute(block, 'beam', ring)  192 us
    pallas_call x9, Pallas kernels, beamform(): pl.pallas_call(functools.partial(beamform_kernel, (n, group, time, own, e...  52.8 us
    ppermute x9, waiting for transfers between devices, over_channels(): lax.ppermute(total, 'chan', [(d, (d + q) % chans) for d in range(chans)])  13.7 us
    ppermute x9, starting transfers between devices, over_channels(): lax.ppermute(total, 'chan', [(d, (d + q) % chans) for d in range(chans)])  12.9 us
    ppermute x9, starting transfers between devices, over_elements(): lax.ppermute(partials[r], 'elem', [(d, (d + r) % elems) for d in range(el...  12.7 us
    ppermute x27, starting transfers between devices, shards(): got = lax.ppermute(block, 'beam', ring)  8.85 us
    unnamed x50, local copies, waits for them, and re-layouts  8.27 us
    ppermute x9, waiting for transfers between devices, over_elements(): lax.ppermute(partials[r], 'elem', [(d, (d + r) % elems) for d in range(el...  6.73 us
  transfers between devices with their start and end apart: 65, of which 32 were waited for; matrix products, arithmetic and copies ran while one was open for 4% of the time, Pallas kernels for 16%

profile of v2, /device:TPU:0, one launch (start us, length us, event | category | flops | bytes accessed | tf_op | source)
XLA Modules:
  0.0 327.9 jit_solution(7161069260314697218)
XLA Ops:
  10.5 8.4 %collective-permute-done.refs_5_ = bf16[2,8,16,1024]{3,2,1,0:T(8,128)(2,1)S(1)} collective-permute-done((bf16[2,8,16,1024]{3,2,1,0:T(8,128)(2,1)S(1)}, bf16[2,8,16,1024]{3,2,1,0:T(8,128)(2,1)S(1)}, u32[]{:S(2)}, u32[]{:S(2)}) %collective-permute-start) | collective-permute-done | bytes 524320 | tf_op jit(solution)/shard_map/ppermute | solution.py:308
  19.0 11.2 %collective-permute-done.2.refs_5_ = bf16[2,8,16,1024]{3,2,1,0:T(8,128)(2,1)S(1)} collective-permute-done((bf16[2,8,16,1024]{3,2,1,0:T(8,128)(2,1)S(1)}, bf16[2,8,16,1024]{3,2,1,0:T(8,128)(2,1)S(1)}, u32[]{:S(2)}, u32[]{:S(2)}) %collective-permute-start.2) | collective-permute-done | bytes 524320 | tf_op jit(solution)/shard_map/ppermute | solution.py:308
  30.2 11.2 %collective-permute-done.1.refs_6_ = bf16[2,8,16,1024]{3,2,1,0:T(8,128)(2,1)S(1)} collective-permute-done((bf16[2,8,16,1024]{3,2,1,0:T(8,128)(2,1)S(1)}, bf16[2,8,16,1024]{3,2,1,0:T(8,128)(2,1)S(1)}, u32[]{:S(2)}, u32[]{:S(2)}) %collective-permute-start.1) | collective-permute-done | bytes 524320 | tf_op jit(solution)/shard_map/ppermute | solution.py:308
  41.4 11.2 %collective-permute-done.3.refs_5_ = bf16[2,8,16,1024]{3,2,1,0:T(8,128)(2,1)S(1)} collective-permute-done((bf16[2,8,16,1024]{3,2,1,0:T(8,128)(2,1)S(1)}, bf16[2,8,16,1024]{3,2,1,0:T(8,128)(2,1)S(1)}, u32[]{:S(2)}, u32[]{:S(2)}) %collective-permute-start.3) | collective-permute-done | bytes 524320 | tf_op jit(solution)/shard_map/ppermute | solution.py:308
  53.7 10.2 %collective-permute-done.10.refs_6_ = bf16[2,8,16,1024]{3,2,1,0:T(8,128)(2,1)S(1)} collective-permute-done((bf16[2,8,16,1024]{3,2,1,0:T(8,128)(2,1)S(1)}, bf16[2,8,16,1024]{3,2,1,0:T(8,128)(2,1)S(1)}, u32[]{:S(2)}, u32[]{:S(2)}) %collective-permute-start.10) | collective-permute-done | bytes 524320 | tf_op jit(solution)/shard_map/ppermute | solution.py:308
  63.9 11.2 %collective-permute-done.4.refs_7_ = bf16[2,8,16,1024]{3,2,1,0:T(8,128)(2,1)S(1)} collective-permute-done((bf16[2,8,16,1024]{3,2,1,0:T(8,128)(2,1)S(1)}, bf16[2,8,16,1024]{3,2,1,0:T(8,128)(2,1)S(1)}, u32[]{:S(2)}, u32[]{:S(2)}) %collective-permute-start.4) | collective-permute-done | bytes 524320 | tf_op jit(solution)/shard_map/ppermute | solution.py:308
  76.3 10.1 %collective-permute-done.11.refs_5_ = bf16[2,8,16,1024]{3,2,1,0:T(8,128)(2,1)S(1)} collective-permute-done((bf16[2,8,16,1024]{3,2,1,0:T(8,128)(2,1)S(1)}, bf16[2,8,16,1024]{3,2,1,0:T(8,128)(2,1)S(1)}, u32[]{:S(2)}, u32[]{:S(2)}) %collective-permute-start.11) | collective-permute-done | bytes 524320 | tf_op jit(solution)/shard_map/ppermute | solution.py:308
  92.6 6.4 %beamform.9 = (bf16[2,32,16,256]{3,2,1,0:T(8,128)(2,1)S(1)}, bf16[2,32,16,256]{3,2,1,0:T(8,128)(2,1)S(1)}) custom-call(s32[12]{0:T(128)S(1)} %stack.51.scalars, bf16[2,64,1024,256]{3,2,1,0:T(8,128)(2,1)} %refs_3_.17, bf16[2,64,1024,256]{3,2,1,0:T(8,128)(2,1)} %refs_3_.17, bf16[2,64,1024,256]{3,2,1,0:T(8,128)(2,1)} %refs_3_.17, ...), custom_call_target="tpu_custom_call" | custom-call | tf_op jit(solution)/shard_map/beamform/pallas_call | solution.py:99
  100.6 8.3 %collective-permute-done.12.refs_7_ = bf16[2,8,16,1024]{3,2,1,0:T(8,128)(2,1)} collective-permute-done((bf16[2,8,16,1024]{3,2,1,0:T(8,128)(2,1)S(1)}, bf16[2,8,16,1024]{3,2,1,0:T(8,128)(2,1)}, u32[]{:S(2)}, u32[]{:S(2)}) %collective-permute-start.12) | collective-permute-done | bytes 524320 | tf_op jit(solution)/shard_map/ppermute | solution.py:308
  109.1 11.0 %collective-permute-done.18.refs_5_ = bf16[2,8,16,1024]{3,2,1,0:T(8,128)(2,1)S(1)} collective-permute-done((bf16[2,8,16,1024]{3,2,1,0:T(8,128)(2,1)S(1)}, bf16[2,8,16,1024]{3,2,1,0:T(8,128)(2,1)S(1)}, u32[]{:S(2)}, u32[]{:S(2)}) %collective-permute-start.18) | collective-permute-done | bytes 524320 | tf_op jit(solution)/shard_map/ppermute | solution.py:308
  121.8 6.5 %beamform.10 = (bf16[2,32,16,256]{3,2,1,0:T(8,128)(2,1)S(1)}, bf16[2,32,16,256]{3,2,1,0:T(8,128)(2,1)S(1)}) custom-call(s32[12]{0:T(128)S(1)} %stack.51.scalars, bf16[2,64,1024,256]{3,2,1,0:T(8,128)(2,1)} %refs_3_.17, bf16[2,64,1024,256]{3,2,1,0:T(8,128)(2,1)} %refs_3_.17, bf16[2,64,1024,256]{3,2,1,0:T(8,128)(2,1)} %refs_3_.17, ...), custom_call_target="tpu_custom_call" | custom-call | tf_op jit(solution)/shard_map/beamform/pallas_call | solution.py:99
  131.3 11.2 %collective-permute-done.19.refs_7_ = bf16[2,8,16,1024]{3,2,1,0:T(8,128)(2,1)S(1)} collective-permute-done((bf16[2,8,16,1024]{3,2,1,0:T(8,128)(2,1)S(1)}, bf16[2,8,16,1024]{3,2,1,0:T(8,128)(2,1)S(1)}, u32[]{:S(2)}, u32[]{:S(2)}) %collective-permute-start.19) | collective-permute-done | bytes 524320 | tf_op jit(solution)/shard_map/ppermute | solution.py:308
  143.2 10.5 %collective-permute-done.25.refs_5_ = bf16[2,8,16,1024]{3,2,1,0:T(8,128)(2,1)S(1)} collective-permute-done((bf16[2,8,16,1024]{3,2,1,0:T(8,128)(2,1)S(1)}, bf16[2,8,16,1024]{3,2,1,0:T(8,128)(2,1)S(1)}, u32[]{:S(2)}, u32[]{:S(2)}) %collective-permute-start.25) | collective-permute-done | bytes 524320 | tf_op jit(solution)/shard_map/ppermute | solution.py:308
  153.8 6.3 %beamform.11 = (bf16[2,32,16,256]{3,2,1,0:T(8,128)(2,1)S(1)}, bf16[2,32,16,256]{3,2,1,0:T(8,128)(2,1)S(1)}) custom-call(s32[12]{0:T(128)S(1)} %stack.51.scalars, bf16[2,64,1024,256]{3,2,1,0:T(8,128)(2,1)} %refs_3_.17, bf16[2,64,1024,256]{3,2,1,0:T(8,128)(2,1)} %refs_3_.17, bf16[2,64,1024,256]{3,2,1,0:T(8,128)(2,1)} %refs_3_.17, ...), custom_call_target="tpu_custom_call" | custom-call | tf_op jit(solution)/shard_map/beamform/pallas_call | solution.py:99
  168.3 7.9 %collective-permute-done.26.refs_7_ = bf16[2,8,16,1024]{3,2,1,0:T(8,128)(2,1)S(1)} collective-permute-done((bf16[2,8,16,1024]{3,2,1,0:T(8,128)(2,1)S(1)}, bf16[2,8,16,1024]{3,2,1,0:T(8,128)(2,1)S(1)}, u32[]{:S(2)}, u32[]{:S(2)}) %collective-permute-start.26) | collective-permute-done | bytes 524320 | tf_op jit(solution)/shard_map/ppermute | solution.py:308
  176.3 11.1 %collective-permute-done.32.refs_5_ = bf16[2,8,16,1024]{3,2,1,0:T(8,128)(2,1)S(1)} collective-permute-done((bf16[2,8,16,1024]{3,2,1,0:T(8,128)(2,1)S(1)}, bf16[2,8,16,1024]{3,2,1,0:T(8,128)(2,1)S(1)}, u32[]{:S(2)}, u32[]{:S(2)}) %collective-permute-start.32) | collective-permute-done | bytes 524320 | tf_op jit(solution)/shard_map/ppermute | solution.py:308
  189.6 6.3 %beamform.12 = (bf16[2,32,16,256]{3,2,1,0:T(8,128)(2,1)S(1)}, bf16[2,32,16,256]{3,2,1,0:T(8,128)(2,1)S(1)}) custom-call(s32[12]{0:T(128)S(1)} %stack.51.scalars, bf16[2,64,1024,256]{3,2,1,0:T(8,128)(2,1)} %refs_3_.17, bf16[2,64,1024,256]{3,2,1,0:T(8,128)(2,1)} %refs_3_.17, bf16[2,64,1024,256]{3,2,1,0:T(8,128)(2,1)} %refs_3_.17, ...), custom_call_target="tpu_custom_call" | custom-call | tf_op jit(solution)/shard_map/beamform/pallas_call | solution.py:99
  195.9 8.0 %collective-permute-done.38.refs_6_ = bf16[2,8,16,1024]{3,2,1,0:T(8,128)(2,1)S(1)} collective-permute-done((bf16[2,8,16,1024]{3,2,1,0:T(8,128)(2,1)S(1)}, bf16[2,8,16,1024]{3,2,1,0:T(8,128)(2,1)S(1)}, u32[]{:S(2)}, u32[]{:S(2)}) %collective-permute-start.38) | collective-permute-done | bytes 524320 | tf_op jit(solution)/shard_map/ppermute | solution.py:308
  205.5 9.7 %collective-permute-done.33.refs_7_ = bf16[2,8,16,1024]{3,2,1,0:T(8,128)(2,1)S(1)} collective-permute-done((bf16[2,8,16,1024]{3,2,1,0:T(8,128)(2,1)S(1)}, bf16[2,8,16,1024]{3,2,1,0:T(8,128)(2,1)S(1)}, u32[]{:S(2)}, u32[]{:S(2)}) %collective-permute-start.33) | collective-permute-done | bytes 524320 | tf_op jit(solution)/shard_map/ppermute | solution.py:308
  215.2 5.5 %collective-permute-done.39.refs_5_ = bf16[2,4,16,1024]{3,2,1,0:T(8,128)(2,1)S(1)} collective-permute-done((bf16[2,4,16,1024]{3,2,1,0:T(8,128)(2,1)S(1)}, bf16[2,4,16,1024]{3,2,1,0:T(8,128)(2,1)S(1)}, u32[]{:S(2)}, u32[]{:S(2)}) %collective-permute-start.39) | collective-permute-done | bytes 262176 | tf_op jit(solution)/shard_map/ppermute | solution.py:308
  228.9 6.3 %beamform.13 = (bf16[2,32,16,256]{3,2,1,0:T(8,128)(2,1)S(1)}, bf16[2,32,16,256]{3,2,1,0:T(8,128)(2,1)S(1)}) custom-call(s32[12]{0:T(128)S(1)} %stack.51.scalars, bf16[2,64,1024,256]{3,2,1,0:T(8,128)(2,1)} %refs_3_.17, bf16[2,64,1024,256]{3,2,1,0:T(8,128)(2,1)} %refs_3_.17, bf16[2,64,1024,256]{3,2,1,0:T(8,128)(2,1)} %refs_3_.17, ...), custom_call_target="tpu_custom_call" | custom-call | tf_op jit(solution)/shard_map/beamform/pallas_call | solution.py:99
  254.1 6.3 %beamform.14 = (bf16[2,32,16,256]{3,2,1,0:T(8,128)(2,1)S(1)}, bf16[2,32,16,256]{3,2,1,0:T(8,128)(2,1)S(1)}) custom-call(s32[12]{0:T(128)S(1)} %stack.51.scalars, bf16[2,64,1024,256]{3,2,1,0:T(8,128)(2,1)} %refs_3_.17, bf16[2,64,1024,256]{3,2,1,0:T(8,128)(2,1)} %refs_3_.17, bf16[2,64,1024,256]{3,2,1,0:T(8,128)(2,1)} %refs_3_.17, ...), custom_call_target="tpu_custom_call" | custom-call | tf_op jit(solution)/shard_map/beamform/pallas_call | solution.py:99
  275.6 7.0 %beamform.15 = (bf16[2,32,16,256]{3,2,1,0:T(8,128)(2,1)S(1)}, bf16[2,32,16,256]{3,2,1,0:T(8,128)(2,1)}) custom-call(s32[12]{0:T(128)S(1)} %stack.51.scalars, bf16[2,64,1024,256]{3,2,1,0:T(8,128)(2,1)} %refs_3_.17, bf16[2,64,1024,256]{3,2,1,0:T(8,128)(2,1)} %refs_3_.17, bf16[2,64,1024,256]{3,2,1,0:T(8,128)(2,1)} %refs_3_.17, ...), custom_call_target="tpu_custom_call" | custom-call | tf_op jit(solution)/shard_map/beamform/pallas_call | solution.py:99
  321.5 6.4 %synthesis.1 = f32[128,32,256]{2,1,0:T(8,128)} custom-call(bf16[768,256]{1,0:T(8,128)(2,1)S(1)} %pad_maximum_fusion.8.table, bf16[2,32,16,256]{3,2,1,0:T(8,128)(2,1)S(1)} %copy-done.4, bf16[2,32,16,256]{3,2,1,0:T(8,128)(2,1)S(1)} %collective-permute-done.8.refs_1_, bf16[32,16,256]{2,1,0:T(8,128)(2,1)S(1)} %copy-done.12, ...), custom_call_target="tpu_custom_call" | custom-call | flops 3221225472 | bytes 12582912 | tf_op jit(solution)/shard_map/synthesis/pallas_call | solution.py:155
  (200 shorter events, 118.9 us)
Async XLA Ops:
  0.0 87.3 %collective-permute-start.5 = (bf16[2,64,16,1024]{3,2,1,0:T(8,128)(2,1)}, bf16[2,64,16,1024]{3,2,1,0:T(8,128)(2,1)}, u32[]{:S(2)}, u32[]{:S(2)}) collective-permute-start(bf16[2,64,16,1024]{3,2,1,0:T(8,128)(2,1)} %refs_4_.17), channel_id=1, source_target_pairs={{0,1},{1,0},{2,3},{3,2},{4,5},{5,4},{6,7},{7,6},{8,9},{9,8},{10,11... | collective-permute-start | bytes 12582920 | tf_op jit(solution)/shard_map/ppermute | solution.py:212
  19.0 22.5 %collective-permute-start.1 = (bf16[2,8,16,1024]{3,2,1,0:T(8,128)(2,1)S(1)}, bf16[2,8,16,1024]{3,2,1,0:T(8,128)(2,1)S(1)}, u32[]{:S(2)}, u32[]{:S(2)}) collective-permute-start(bf16[2,8,16,1024]{3,2,1,0:T(8,128)(2,1)S(1)} %collective-permute-done.refs_5_), channel_id=1, source_target_pairs={{0,2},{1,3},{2,4},{3,5},{4,6},{5,7},{6,0},{7,1},{8,10},{9,11},{10,... | collective-permute-start | bytes 1572872 | tf_op jit(solution)/shard_map/ppermute | solution.py:308
  30.2 22.5 %collective-permute-start.3 = (bf16[2,8,16,1024]{3,2,1,0:T(8,128)(2,1)S(1)}, bf16[2,8,16,1024]{3,2,1,0:T(8,128)(2,1)S(1)}, u32[]{:S(2)}, u32[]{:S(2)}) collective-permute-start(bf16[2,8,16,1024]{3,2,1,0:T(8,128)(2,1)S(1)} %get-tuple-element.62), channel_id=1, source_target_pairs={{0,2},{1,3},{2,4},{3,5},{4,6},{5,7},{6,0},{7,1},{8,10},{9,11},{10,... | collective-permute-start | bytes 1572872 | tf_op jit(solution)/shard_map/ppermute | solution.py:308
  41.4 22.5 %collective-permute-start.10 = (bf16[2,8,16,1024]{3,2,1,0:T(8,128)(2,1)S(1)}, bf16[2,8,16,1024]{3,2,1,0:T(8,128)(2,1)S(1)}, u32[]{:S(2)}, u32[]{:S(2)}) collective-permute-start(bf16[2,8,16,1024]{3,2,1,0:T(8,128)(2,1)S(1)} %collective-permute-done.2.refs_5_), channel_id=1, source_target_pairs={{0,2},{1,3},{2,4},{3,5},{4,6},{5,7},{6,0},{7,1},{8,10},{9,11},{10,... | collective-permute-start | bytes 1572872 | tf_op jit(solution)/shard_map/ppermute | solution.py:308
  52.7 22.5 %collective-permute-start.4 = (bf16[2,8,16,1024]{3,2,1,0:T(8,128)(2,1)S(1)}, bf16[2,8,16,1024]{3,2,1,0:T(8,128)(2,1)S(1)}, u32[]{:S(2)}, u32[]{:S(2)}) collective-permute-start(bf16[2,8,16,1024]{3,2,1,0:T(8,128)(2,1)S(1)} %collective-permute-done.1.refs_6_), channel_id=1, source_target_pairs={{0,2},{1,3},{2,4},{3,5},{4,6},{5,7},{6,0},{7,1},{8,10},{9,11},{10,... | collective-permute-start | bytes 1572872 | tf_op jit(solution)/shard_map/ppermute | solution.py:308
  53.7 33.5 %collective-permute-start.6 = (bf16[4,8,16,1024]{3,2,1,0:T(8,128)(2,1)}, bf16[4,8,16,1024]{3,2,1,0:T(8,128)(2,1)}, u32[]{:S(2)}, u32[]{:S(2)}) collective-permute-start(bf16[4,8,16,1024]{3,2,1,0:T(8,128)(2,1)} %pad_maximum_fusion), channel_id=1, source_target_pairs={{0,1},{1,0},{2,3},{3,2},{4,5},{5,4},{6,7},{7,6},{8,9},{9,8},{10,11... | collective-permute-start | bytes 3145736 | tf_op jit(solution)/shard_map/ppermute | solution.py:240
  63.9 22.5 %collective-permute-start.11 = (bf16[2,8,16,1024]{3,2,1,0:T(8,128)(2,1)S(1)}, bf16[2,8,16,1024]{3,2,1,0:T(8,128)(2,1)S(1)}, u32[]{:S(2)}, u32[]{:S(2)}) collective-permute-start(bf16[2,8,16,1024]{3,2,1,0:T(8,128)(2,1)S(1)} %get-tuple-element.67), channel_id=1, source_target_pairs={{0,2},{1,3},{2,4},{3,5},{4,6},{5,7},{6,0},{7,1},{8,10},{9,11},{10,... | collective-permute-start | bytes 1572872 | tf_op jit(solution)/shard_map/ppermute | solution.py:308
  75.2 23.9 %collective-permute-start.17 = (bf16[2,8,16,1024]{3,2,1,0:T(8,128)(2,1)S(1)}, bf16[2,8,16,1024]{3,2,1,0:T(8,128)(2,1)S(1)}, u32[]{:S(2)}, u32[]{:S(2)}) collective-permute-start(bf16[2,8,16,1024]{3,2,1,0:T(8,128)(2,1)S(1)} %collective-permute-done.3.refs_5_), channel_id=1, source_target_pairs={{0,2},{1,3},{2,4},{3,5},{4,6},{5,7},{6,0},{7,1},{8,10},{9,11},{10,... | collective-permute-start | bytes 1572872 | tf_op jit(solution)/shard_map/ppermute | solution.py:308
  86.4 22.6 %collective-permute-start.12 = (bf16[2,8,16,1024]{3,2,1,0:T(8,128)(2,1)S(1)}, bf16[2,8,16,1024]{3,2,1,0:T(8,128)(2,1)}, u32[]{:S(2)}, u32[]{:S(2)}) collective-permute-start(bf16[2,8,16,1024]{3,2,1,0:T(8,128)(2,1)S(1)} %collective-permute-done.10.refs_6_), channel_id=1, source_target_pairs={{0,2},{1,3},{2,4},{3,5},{4,6},{5,7},{6,0},{7,1},{8,10},{9,11},{10,... | collective-permute-start | bytes 1572872 | tf_op jit(solution)/shard_map/ppermute | solution.py:308
  87.2 32.9 %collective-permute-start.13 = (bf16[4,8,16,1024]{3,2,1,0:T(8,128)(2,1)}, bf16[4,8,16,1024]{3,2,1,0:T(8,128)(2,1)}, u32[]{:S(2)}, u32[]{:S(2)}) collective-permute-start(bf16[4,8,16,1024]{3,2,1,0:T(8,128)(2,1)} %pad_maximum_fusion.1), channel_id=1, source_target_pairs={{0,1},{1,0},{2,3},{3,2},{4,5},{5,4},{6,7},{7,6},{8,9},{9,8},{10,11... | collective-permute-start | bytes 3145736 | tf_op jit(solution)/shard_map/ppermute | solution.py:240
  109.0 22.4 %collective-permute-start.24 = (bf16[2,8,16,1024]{3,2,1,0:T(8,128)(2,1)S(1)}, bf16[2,8,16,1024]{3,2,1,0:T(8,128)(2,1)S(1)}, u32[]{:S(2)}, u32[]{:S(2)}) collective-permute-start(bf16[2,8,16,1024]{3,2,1,0:T(8,128)(2,1)S(1)} %collective-permute-done.11.refs_5_), channel_id=1, source_target_pairs={{0,2},{1,3},{2,4},{3,5},{4,6},{5,7},{6,0},{7,1},{8,10},{9,11},{10,... | collective-permute-start | bytes 1572872 | tf_op jit(solution)/shard_map/ppermute | solution.py:308
  120.1 22.5 %collective-permute-start.19 = (bf16[2,8,16,1024]{3,2,1,0:T(8,128)(2,1)S(1)}, bf16[2,8,16,1024]{3,2,1,0:T(8,128)(2,1)S(1)}, u32[]{:S(2)}, u32[]{:S(2)}) collective-permute-start(bf16[2,8,16,1024]{3,2,1,0:T(8,128)(2,1)S(1)} %collective-permute-done.17.refs_6_), channel_id=1, source_target_pairs={{0,2},{1,3},{2,4},{3,5},{4,6},{5,7},{6,0},{7,1},{8,10},{9,11},{10,... | collective-permute-start | bytes 1572872 | tf_op jit(solution)/shard_map/ppermute | solution.py:308
  120.1 33.7 %collective-permute-start.20 = (bf16[4,8,16,1024]{3,2,1,0:T(8,128)(2,1)S(1)}, bf16[4,8,16,1024]{3,2,1,0:T(8,128)(2,1)S(1)}, u32[]{:S(2)}, u32[]{:S(2)}) collective-permute-start(bf16[4,8,16,1024]{3,2,1,0:T(8,128)(2,1)S(1)} %pad_maximum_fusion.2), channel_id=1, source_target_pairs={{0,1},{1,0},{2,3},{3,2},{4,5},{5,4},{6,7},{7,6},{8,9},{9,8},{10,11... | collective-permute-start | bytes 3145736 | tf_op jit(solution)/shard_map/ppermute | solution.py:240
  120.1 22.5 %collective-permute-start.8 = (bf16[2,32,16,256]{3,2,1,0:T(8,128)(2,1)S(1)}, bf16[2,32,16,256]{3,2,1,0:T(8,128)(2,1)S(1)}, u32[]{:S(2)}, u32[]{:S(2)}) collective-permute-start(bf16[2,32,16,256]{3,2,1,0:T(8,128)(2,1)S(1)} %get-tuple-element.65), channel_id=1, source_target_pairs={{0,8},{8,0},{1,9},{9,1},{2,10},{10,2},{3,11},{11,3},{4,12},{12,4},... | collective-permute-start | bytes 1572872 | tf_op jit(solution)/shard_map/ppermute | solution.py:248
  131.3 22.5 %collective-permute-start.25 = (bf16[2,8,16,1024]{3,2,1,0:T(8,128)(2,1)S(1)}, bf16[2,8,16,1024]{3,2,1,0:T(8,128)(2,1)S(1)}, u32[]{:S(2)}, u32[]{:S(2)}) collective-permute-start(bf16[2,8,16,1024]{3,2,1,0:T(8,128)(2,1)S(1)} %copy-done.22), channel_id=1, source_target_pairs={{0,2},{1,3},{2,4},{3,5},{4,6},{5,7},{6,0},{7,1},{8,10},{9,11},{10,... | collective-permute-start | bytes 1572872 | tf_op jit(solution)/shard_map/ppermute | solution.py:308
  142.6 22.5 %collective-permute-start.31 = (bf16[2,8,16,1024]{3,2,1,0:T(8,128)(2,1)S(1)}, bf16[2,8,16,1024]{3,2,1,0:T(8,128)(2,1)S(1)}, u32[]{:S(2)}, u32[]{:S(2)}) collective-permute-start(bf16[2,8,16,1024]{3,2,1,0:T(8,128)(2,1)S(1)} %collective-permute-done.18.refs_5_), channel_id=1, source_target_pairs={{0,2},{1,3},{2,4},{3,5},{4,6},{5,7},{6,0},{7,1},{8,10},{9,11},{10,... | collective-permute-start | bytes 1572872 | tf_op jit(solution)/shard_map/ppermute | solution.py:308
  142.7 46.9 %collective-permute-start.27 = (bf16[4,8,16,1024]{3,2,1,0:T(8,128)(2,1)S(1)}, bf16[4,8,16,1024]{3,2,1,0:T(8,128)(2,1)S(1)}, u32[]{:S(2)}, u32[]{:S(2)}) collective-permute-start(bf16[4,8,16,1024]{3,2,1,0:T(8,128)(2,1)S(1)} %pad_maximum_fusion.3), channel_id=1, source_target_pairs={{0,1},{1,0},{2,3},{3,2},{4,5},{5,4},{6,7},{7,6},{8,9},{9,8},{10,11... | collective-permute-start | bytes 3145736 | tf_op jit(solution)/shard_map/ppermute | solution.py:240
  153.8 22.5 %collective-permute-start.26 = (bf16[2,8,16,1024]{3,2,1,0:T(8,128)(2,1)S(1)}, bf16[2,8,16,1024]{3,2,1,0:T(8,128)(2,1)S(1)}, u32[]{:S(2)}, u32[]{:S(2)}) collective-permute-start(bf16[2,8,16,1024]{3,2,1,0:T(8,128)(2,1)S(1)} %collective-permute-done.24.refs_6_), channel_id=1, source_target_pairs={{0,2},{1,3},{2,4},{3,5},{4,6},{5,7},{6,0},{7,1},{8,10},{9,11},{10,... | collective-permute-start | bytes 1572872 | tf_op jit(solution)/shard_map/ppermute | solution.py:308
  187.3 27.8 %collective-permute-start.33 = (bf16[2,8,16,1024]{3,2,1,0:T(8,128)(2,1)S(1)}, bf16[2,8,16,1024]{3,2,1,0:T(8,128)(2,1)S(1)}, u32[]{:S(2)}, u32[]{:S(2)}) collective-permute-start(bf16[2,8,16,1024]{3,2,1,0:T(8,128)(2,1)S(1)} %collective-permute-done.31.refs_6_), channel_id=1, source_target_pairs={{0,2},{1,3},{2,4},{3,5},{4,6},{5,7},{6,0},{7,1},{8,10},{9,11},{10,... | collective-permute-start | bytes 1572872 | tf_op jit(solution)/shard_map/ppermute | solution.py:308
  188.7 40.2 %collective-permute-start.34 = (bf16[4,8,16,1024]{3,2,1,0:T(8,128)(2,1)S(1)}, bf16[4,8,16,1024]{3,2,1,0:T(8,128)(2,1)S(1)}, u32[]{:S(2)}, u32[]{:S(2)}) collective-permute-start(bf16[4,8,16,1024]{3,2,1,0:T(8,128)(2,1)S(1)} %pad_maximum_fusion.4), channel_id=1, source_target_pairs={{0,1},{1,0},{2,3},{3,2},{4,5},{5,4},{6,7},{7,6},{8,9},{9,8},{10,11... | collective-permute-start | bytes 3145736 | tf_op jit(solution)/shard_map/ppermute | solution.py:240
  203.9 25.0 %collective-permute-start.22 = (bf16[2,32,16,256]{3,2,1,0:T(8,128)(2,1)S(1)}, bf16[2,32,16,256]{3,2,1,0:T(8,128)(2,1)S(1)}, u32[]{:S(2)}, u32[]{:S(2)}) collective-permute-start(bf16[2,32,16,256]{3,2,1,0:T(8,128)(2,1)S(1)} %get-tuple-element.76), channel_id=1, source_target_pairs={{0,8},{8,0},{1,9},{9,1},{2,10},{10,2},{3,11},{11,3},{4,12},{12,4},... | collective-permute-start | bytes 1572872 | tf_op jit(solution)/shard_map/ppermute | solution.py:248
  228.9 23.6 %collective-permute-start.41 = (bf16[4,8,16,1024]{3,2,1,0:T(8,128)(2,1)}, bf16[4,8,16,1024]{3,2,1,0:T(8,128)(2,1)S(1)}, u32[]{:S(2)}, u32[]{:S(2)}) collective-permute-start(bf16[4,8,16,1024]{3,2,1,0:T(8,128)(2,1)} %pad_maximum_fusion.5), channel_id=1, source_target_pairs={{0,1},{1,0},{2,3},{3,2},{4,5},{5,4},{6,7},{7,6},{8,9},{9,8},{10,11... | collective-permute-start | bytes 3145736 | tf_op jit(solution)/shard_map/ppermute | solution.py:240
  243.9 30.2 %collective-permute-start.48 = (bf16[4,8,16,1024]{3,2,1,0:T(8,128)(2,1)S(1)}, bf16[4,8,16,1024]{3,2,1,0:T(8,128)(2,1)S(1)}, u32[]{:S(2)}, u32[]{:S(2)}) collective-permute-start(bf16[4,8,16,1024]{3,2,1,0:T(8,128)(2,1)S(1)} %pad_maximum_fusion.6), channel_id=1, source_target_pairs={{0,1},{1,0},{2,3},{3,2},{4,5},{5,4},{6,7},{7,6},{8,9},{9,8},{10,11... | collective-permute-start | bytes 3145736 | tf_op jit(solution)/shard_map/ppermute | solution.py:240
  251.0 22.9 %collective-permute-start.36 = (bf16[2,32,16,256]{3,2,1,0:T(8,128)(2,1)S(1)}, bf16[2,32,16,256]{3,2,1,0:T(8,128)(2,1)S(1)}, u32[]{:S(2)}, u32[]{:S(2)}) collective-permute-start(bf16[2,32,16,256]{3,2,1,0:T(8,128)(2,1)S(1)} %get-tuple-element.88), channel_id=1, source_target_pairs={{0,8},{8,0},{1,9},{9,1},{2,10},{10,2},{3,11},{11,3},{4,12},{12,4},... | collective-permute-start | bytes 1572872 | tf_op jit(solution)/shard_map/ppermute | solution.py:248
  (66 other events, 966.5 us)

commit v3 on v2

--- a/solution.py
+++ b/solution.py
@@ -12,10 +12,11 @@
 BF16 = jnp.bfloat16
 VMEM_BYTES = 40 * 2**20
 WINDOW = (2,)
-Y_LAG, X_LAG, RING_LAG, UNGATED = 2, 3, 0, 1
+Y_LAG, X_LAG, RING_LAG, UNGATED = 2, 2, 0, 1
 FLOPS = 0
 TAIL_GATE = 3
 TABLE_SLOT = 1
+FREE = 0
 SKEW, SPLIT_SWAPS = 1, 1
 CUTS = 2
 GROUP = 4
@@ -106,7 +107,7 @@
             out_specs=[pl.BlockSpec(shape, lambda i, s: (0, 0, 0, 0))] * elems,
             scratch_shapes=[
                 pltpu.VMEM((group, 2 * time, depth), BF16),
-                pltpu.VMEM((beams // lanes, time * 2 * n, lanes), F32),
+                pltpu.VMEM((beams // lanes, (time + 1) * 2 * n, lanes), F32),
             ],
         ),
         compiler_params=pltpu.CompilerParams(vmem_limit_bytes=VMEM_BYTES),
@@ -120,9 +121,8 @@
 
 
 def synthesis_kernel(layout, channels, table, *refs):
-    out = refs[-1]
+    out, rows_of = refs[-2:]
     times, beams = out.shape[1], out.shape[2]
-    flat = out.reshape(channels * times, beams)
     lanes = min(128, beams)
     for t in range(times):
         rows, at = [], 0
@@ -139,7 +139,11 @@
         parts = jnp.dot(table[...], held, preferred_element_type=F32)
         half = 2 * channels
         fine = parts[:half] + (parts[half : 2 * half] + parts[2 * half :])
-        out[:, t, :] = fine[:channels] * fine[:channels] + fine[channels:] * fine[channels:]
+        power = fine[:channels] * fine[:channels] + fine[channels:] * fine[channels:]
+        for j in range(beams // lanes):
+            rows_of[j, pl.ds(t, channels, stride=times), :] = power[:, j * lanes : (j + 1) * lanes]
+    for j in range(beams // lanes):
+        out[:, :, j * lanes : (j + 1) * lanes] = rows_of[j, : channels * times].reshape(channels, times, lanes)
 
 
 def synthesis(table, groups, channels, own, beams):
@@ -158,6 +162,7 @@
         grid=(own // times,),
         in_specs=in_specs,
         out_specs=pl.BlockSpec((channels, times, beams), lambda i: (0, i, 0)),
+        scratch_shapes=[pltpu.VMEM((beams // min(128, beams), (channels + 1) * times, min(128, beams)), F32)],
         compiler_params=pltpu.CompilerParams(vmem_limit_bytes=VMEM_BYTES),
         cost_estimate=pl.CostEstimate(
             flops=24 * channels * channels * own * beams,
@@ -293,7 +298,7 @@
         waits = []
         if 0 <= slot - depth - 1 < count:
             work_on(slot - depth - 1)
-        if 0 <= slot - depth - 1 - RING_LAG < count:
+        if 0 <= slot - depth - 1 - RING_LAG < count - FREE:
             waits.append(partials[slot - depth - 1 - RING_LAG][-1])
         if slot == TABLE_SLOT:
             waits.append(table)

time: 328 us -> 320 us (0.976)
  waiting for transfers between devices: 212 us -> 204 us
    ppermute x27, waiting for transfers between devices: 192 us -> 183 us  [shards(): got = lax.ppermute(block, 'beam', ring)]
    ppermute x9, waiting for transfers between devices: 6.73 us -> 10.3 us  [over_elements(): lax.ppermute(partials[r], 'elem', [(d, (d + r) % elems) for d in range(el...]
    unnamed x50 -> x90, local copies, waits for them, and re-layouts: 8.27 us -> 8.36 us
  transfers between devices with their start and end apart: 65 -> 65, of which waited for: 32 -> 33; matrix products, arithmetic and copies ran while one was open for 4% -> 3% of each run, Pallas kernels for 16% -> 17%
where the time goes in v3:
time: 320 us
  waiting for transfers between devices  204 us (64%)
  Pallas kernels  59.2 us (18%)
  starting transfers between devices  36 us (11%)
  local copies, waits for them, and re-layouts  13.6 us (4%)
  other arithmetic  5.55 us (2%)
    ppermute x27, waiting for transfers between devices, shards(): got = lax.ppermute(block, 'beam', ring)  183 us
    pallas_call x9, Pallas kernels, beamform(): pl.pallas_call(functools.partial(beamform_kernel, (n, group, time, own, e...  52.9 us
    ppermute x9, starting transfers between devices, over_elements(): lax.ppermute(partials[r], 'elem', [(d, (d + r) % elems) for d in range(el...  13.4 us
    ppermute x9, starting transfers between devices, over_channels(): lax.ppermute(total, 'chan', [(d, (d + q) % chans) for d in range(chans)])  12.2 us
    ppermute x9, waiting for transfers between devices, over_channels(): lax.ppermute(total, 'chan', [(d, (d + q) % chans) for d in range(chans)])  11.3 us
    ppermute x9, waiting for transfers between devices, over_elements(): lax.ppermute(partials[r], 'elem', [(d, (d + r) % elems) for d in range(el...  10.3 us
    ppermute x27, starting transfers between devices, shards(): got = lax.ppermute(block, 'beam', ring)  8.59 us
    unnamed x90, local copies, waits for them, and re-layouts  8.36 us
  transfers between devices with their start and end apart: 65, of which 33 were waited for; matrix products, arithmetic and copies ran while one was open for 3% of the time, Pallas kernels for 17%

profile of v3, /device:TPU:0, one launch (start us, length us, event | category | flops | bytes accessed | tf_op | source)
XLA Modules:
  0.0 319.6 jit_solution(1647143757731729365)
XLA Ops:
  10.5 8.4 %collective-permute-done.refs_5_ = bf16[2,8,16,1024]{3,2,1,0:T(8,128)(2,1)S(1)} collective-permute-done((bf16[2,8,16,1024]{3,2,1,0:T(8,128)(2,1)S(1)}, bf16[2,8,16,1024]{3,2,1,0:T(8,128)(2,1)S(1)}, u32[]{:S(2)}, u32[]{:S(2)}) %collective-permute-start) | collective-permute-done | bytes 524320 | tf_op jit(solution)/shard_map/ppermute | solution.py:313
  19.0 11.2 %collective-permute-done.2.refs_5_ = bf16[2,8,16,1024]{3,2,1,0:T(8,128)(2,1)S(1)} collective-permute-done((bf16[2,8,16,1024]{3,2,1,0:T(8,128)(2,1)S(1)}, bf16[2,8,16,1024]{3,2,1,0:T(8,128)(2,1)S(1)}, u32[]{:S(2)}, u32[]{:S(2)}) %collective-permute-start.2) | collective-permute-done | bytes 524320 | tf_op jit(solution)/shard_map/ppermute | solution.py:313
  30.2 11.2 %collective-permute-done.1.refs_6_ = bf16[2,8,16,1024]{3,2,1,0:T(8,128)(2,1)S(1)} collective-permute-done((bf16[2,8,16,1024]{3,2,1,0:T(8,128)(2,1)S(1)}, bf16[2,8,16,1024]{3,2,1,0:T(8,128)(2,1)S(1)}, u32[]{:S(2)}, u32[]{:S(2)}) %collective-permute-start.1) | collective-permute-done | bytes 524320 | tf_op jit(solution)/shard_map/ppermute | solution.py:313
  41.4 11.2 %collective-permute-done.3.refs_5_ = bf16[2,8,16,1024]{3,2,1,0:T(8,128)(2,1)S(1)} collective-permute-done((bf16[2,8,16,1024]{3,2,1,0:T(8,128)(2,1)S(1)}, bf16[2,8,16,1024]{3,2,1,0:T(8,128)(2,1)S(1)}, u32[]{:S(2)}, u32[]{:S(2)}) %collective-permute-start.3) | collective-permute-done | bytes 524320 | tf_op jit(solution)/shard_map/ppermute | solution.py:313
  53.7 10.2 %collective-permute-done.10.refs_6_ = bf16[2,8,16,1024]{3,2,1,0:T(8,128)(2,1)S(1)} collective-permute-done((bf16[2,8,16,1024]{3,2,1,0:T(8,128)(2,1)S(1)}, bf16[2,8,16,1024]{3,2,1,0:T(8,128)(2,1)S(1)}, u32[]{:S(2)}, u32[]{:S(2)}) %collective-permute-start.10) | collective-permute-done | bytes 524320 | tf_op jit(solution)/shard_map/ppermute | solution.py:313
  63.9 11.2 %collective-permute-done.4.refs_7_ = bf16[2,8,16,1024]{3,2,1,0:T(8,128)(2,1)S(1)} collective-permute-done((bf16[2,8,16,1024]{3,2,1,0:T(8,128)(2,1)S(1)}, bf16[2,8,16,1024]{3,2,1,0:T(8,128)(2,1)S(1)}, u32[]{:S(2)}, u32[]{:S(2)}) %collective-permute-start.4) | collective-permute-done | bytes 524320 | tf_op jit(solution)/shard_map/ppermute | solution.py:313
  76.3 10.0 %collective-permute-done.11.refs_5_ = bf16[2,8,16,1024]{3,2,1,0:T(8,128)(2,1)S(1)} collective-permute-done((bf16[2,8,16,1024]{3,2,1,0:T(8,128)(2,1)S(1)}, bf16[2,8,16,1024]{3,2,1,0:T(8,128)(2,1)S(1)}, u32[]{:S(2)}, u32[]{:S(2)}) %collective-permute-start.11) | collective-permute-done | bytes 524320 | tf_op jit(solution)/shard_map/ppermute | solution.py:313
  92.6 6.4 %beamform.9 = (bf16[2,32,16,256]{3,2,1,0:T(8,128)(2,1)S(1)}, bf16[2,32,16,256]{3,2,1,0:T(8,128)(2,1)S(1)}) custom-call(s32[12]{0:T(128)S(1)} %stack.51.scalars, bf16[2,64,1024,256]{3,2,1,0:T(8,128)(2,1)} %refs_3_.17, bf16[2,64,1024,256]{3,2,1,0:T(8,128)(2,1)} %refs_3_.17, bf16[2,64,1024,256]{3,2,1,0:T(8,128)(2,1)} %refs_3_.17, ...), custom_call_target="tpu_custom_call" | custom-call | tf_op jit(solution)/shard_map/beamform/pallas_call | solution.py:100
  100.7 8.3 %collective-permute-done.12.refs_7_ = bf16[2,8,16,1024]{3,2,1,0:T(8,128)(2,1)} collective-permute-done((bf16[2,8,16,1024]{3,2,1,0:T(8,128)(2,1)S(1)}, bf16[2,8,16,1024]{3,2,1,0:T(8,128)(2,1)}, u32[]{:S(2)}, u32[]{:S(2)}) %collective-permute-start.12) | collective-permute-done | bytes 524320 | tf_op jit(solution)/shard_map/ppermute | solution.py:313
  109.6 10.4 %collective-permute-done.18.refs_5_ = bf16[2,8,16,1024]{3,2,1,0:T(8,128)(2,1)S(1)} collective-permute-done((bf16[2,8,16,1024]{3,2,1,0:T(8,128)(2,1)S(1)}, bf16[2,8,16,1024]{3,2,1,0:T(8,128)(2,1)S(1)}, u32[]{:S(2)}, u32[]{:S(2)}) %collective-permute-start.18) | collective-permute-done | bytes 524320 | tf_op jit(solution)/shard_map/ppermute | solution.py:313
  121.7 6.5 %beamform.10 = (bf16[2,32,16,256]{3,2,1,0:T(8,128)(2,1)S(1)}, bf16[2,32,16,256]{3,2,1,0:T(8,128)(2,1)S(1)}) custom-call(s32[12]{0:T(128)S(1)} %stack.51.scalars, bf16[2,64,1024,256]{3,2,1,0:T(8,128)(2,1)} %refs_3_.17, bf16[2,64,1024,256]{3,2,1,0:T(8,128)(2,1)} %refs_3_.17, bf16[2,64,1024,256]{3,2,1,0:T(8,128)(2,1)} %refs_3_.17, ...), custom_call_target="tpu_custom_call" | custom-call | tf_op jit(solution)/shard_map/beamform/pallas_call | solution.py:100
  131.3 11.2 %collective-permute-done.19.refs_7_ = bf16[2,8,16,1024]{3,2,1,0:T(8,128)(2,1)S(1)} collective-permute-done((bf16[2,8,16,1024]{3,2,1,0:T(8,128)(2,1)S(1)}, bf16[2,8,16,1024]{3,2,1,0:T(8,128)(2,1)S(1)}, u32[]{:S(2)}, u32[]{:S(2)}) %collective-permute-start.19) | collective-permute-done | bytes 524320 | tf_op jit(solution)/shard_map/ppermute | solution.py:313
  146.1 7.7 %collective-permute-done.25.refs_5_ = bf16[2,8,16,1024]{3,2,1,0:T(8,128)(2,1)S(1)} collective-permute-done((bf16[2,8,16,1024]{3,2,1,0:T(8,128)(2,1)S(1)}, bf16[2,8,16,1024]{3,2,1,0:T(8,128)(2,1)S(1)}, u32[]{:S(2)}, u32[]{:S(2)}) %collective-permute-start.25) | collective-permute-done | bytes 524320 | tf_op jit(solution)/shard_map/ppermute | solution.py:313
  155.1 6.3 %beamform.11 = (bf16[2,32,16,256]{3,2,1,0:T(8,128)(2,1)S(1)}, bf16[2,32,16,256]{3,2,1,0:T(8,128)(2,1)S(1)}) custom-call(s32[12]{0:T(128)S(1)} %stack.51.scalars, bf16[2,64,1024,256]{3,2,1,0:T(8,128)(2,1)} %refs_3_.17, bf16[2,64,1024,256]{3,2,1,0:T(8,128)(2,1)} %refs_3_.17, bf16[2,64,1024,256]{3,2,1,0:T(8,128)(2,1)} %refs_3_.17, ...), custom_call_target="tpu_custom_call" | custom-call | tf_op jit(solution)/shard_map/beamform/pallas_call | solution.py:100
  167.0 9.3 %collective-permute-done.26.refs_7_ = bf16[2,8,16,1024]{3,2,1,0:T(8,128)(2,1)S(1)} collective-permute-done((bf16[2,8,16,1024]{3,2,1,0:T(8,128)(2,1)S(1)}, bf16[2,8,16,1024]{3,2,1,0:T(8,128)(2,1)S(1)}, u32[]{:S(2)}, u32[]{:S(2)}) %collective-permute-start.26) | collective-permute-done | bytes 524320 | tf_op jit(solution)/shard_map/ppermute | solution.py:313
  177.0 10.5 %collective-permute-done.32.refs_5_ = bf16[2,8,16,1024]{3,2,1,0:T(8,128)(2,1)S(1)} collective-permute-done((bf16[2,8,16,1024]{3,2,1,0:T(8,128)(2,1)S(1)}, bf16[2,8,16,1024]{3,2,1,0:T(8,128)(2,1)S(1)}, u32[]{:S(2)}, u32[]{:S(2)}) %collective-permute-start.32) | collective-permute-done | bytes 524320 | tf_op jit(solution)/shard_map/ppermute | solution.py:313
  189.9 6.3 %beamform.12 = (bf16[2,32,16,256]{3,2,1,0:T(8,128)(2,1)S(1)}, bf16[2,32,16,256]{3,2,1,0:T(8,128)(2,1)S(1)}) custom-call(s32[12]{0:T(128)S(1)} %stack.51.scalars, bf16[2,64,1024,256]{3,2,1,0:T(8,128)(2,1)} %refs_3_.17, bf16[2,64,1024,256]{3,2,1,0:T(8,128)(2,1)} %refs_3_.17, bf16[2,64,1024,256]{3,2,1,0:T(8,128)(2,1)} %refs_3_.17, ...), custom_call_target="tpu_custom_call" | custom-call | tf_op jit(solution)/shard_map/beamform/pallas_call | solution.py:100
  202.6 7.4 %collective-permute-done.33.refs_7_ = bf16[2,8,16,1024]{3,2,1,0:T(8,128)(2,1)S(1)} collective-permute-done((bf16[2,8,16,1024]{3,2,1,0:T(8,128)(2,1)S(1)}, bf16[2,8,16,1024]{3,2,1,0:T(8,128)(2,1)S(1)}, u32[]{:S(2)}, u32[]{:S(2)}) %collective-permute-start.33) | collective-permute-done | bytes 524320 | tf_op jit(solution)/shard_map/ppermute | solution.py:313
  218.1 6.3 %beamform.13 = (bf16[2,32,16,256]{3,2,1,0:T(8,128)(2,1)S(1)}, bf16[2,32,16,256]{3,2,1,0:T(8,128)(2,1)S(1)}) custom-call(s32[12]{0:T(128)S(1)} %stack.51.scalars, bf16[2,64,1024,256]{3,2,1,0:T(8,128)(2,1)} %refs_3_.17, bf16[2,64,1024,256]{3,2,1,0:T(8,128)(2,1)} %refs_3_.17, bf16[2,64,1024,256]{3,2,1,0:T(8,128)(2,1)} %refs_3_.17, ...), custom_call_target="tpu_custom_call" | custom-call | tf_op jit(solution)/shard_map/beamform/pallas_call | solution.py:100
  230.7 7.4 %collective-permute-done.40.refs_7_ = bf16[2,8,16,1024]{3,2,1,0:T(8,128)(2,1)S(1)} collective-permute-done((bf16[2,8,16,1024]{3,2,1,0:T(8,128)(2,1)S(1)}, bf16[2,8,16,1024]{3,2,1,0:T(8,128)(2,1)S(1)}, u32[]{:S(2)}, u32[]{:S(2)}) %collective-permute-start.40) | collective-permute-done | bytes 524320 | tf_op jit(solution)/shard_map/ppermute | solution.py:313
  245.2 6.3 %beamform.14 = (bf16[2,32,16,256]{3,2,1,0:T(8,128)(2,1)S(1)}, bf16[2,32,16,256]{3,2,1,0:T(8,128)(2,1)S(1)}) custom-call(s32[12]{0:T(128)S(1)} %stack.51.scalars, bf16[2,64,1024,256]{3,2,1,0:T(8,128)(2,1)} %refs_3_.17, bf16[2,64,1024,256]{3,2,1,0:T(8,128)(2,1)} %refs_3_.17, bf16[2,64,1024,256]{3,2,1,0:T(8,128)(2,1)} %refs_3_.17, ...), custom_call_target="tpu_custom_call" | custom-call | tf_op jit(solution)/shard_map/beamform/pallas_call | solution.py:100
  253.4 6.7 %collective-permute-done.47.refs_7_ = bf16[2,8,16,1024]{3,2,1,0:T(8,128)(2,1)S(1)} collective-permute-done((bf16[2,8,16,1024]{3,2,1,0:T(8,128)(2,1)S(1)}, bf16[2,8,16,1024]{3,2,1,0:T(8,128)(2,1)S(1)}, u32[]{:S(2)}, u32[]{:S(2)}) %collective-permute-start.47) | collective-permute-done | bytes 524320 | tf_op jit(solution)/shard_map/ppermute | solution.py:313
  270.9 7.0 %beamform.15 = (bf16[2,32,16,256]{3,2,1,0:T(8,128)(2,1)S(1)}, bf16[2,32,16,256]{3,2,1,0:T(8,128)(2,1)}) custom-call(s32[12]{0:T(128)S(1)} %stack.51.scalars, bf16[2,64,1024,256]{3,2,1,0:T(8,128)(2,1)} %refs_3_.17, bf16[2,64,1024,256]{3,2,1,0:T(8,128)(2,1)} %refs_3_.17, bf16[2,64,1024,256]{3,2,1,0:T(8,128)(2,1)} %refs_3_.17, ...), custom_call_target="tpu_custom_call" | custom-call | tf_op jit(solution)/shard_map/beamform/pallas_call | solution.py:100
  313.3 6.3 %synthesis.1 = f32[128,32,256]{2,1,0:T(8,128)} custom-call(bf16[768,256]{1,0:T(8,128)(2,1)S(1)} %pad_maximum_fusion.8.table, bf16[2,32,16,256]{3,2,1,0:T(8,128)(2,1)S(1)} %copy-done.4, bf16[2,32,16,256]{3,2,1,0:T(8,128)(2,1)S(1)} %copy-done.6, bf16[32,16,256]{2,1,0:T(8,128)(2,1)S(1)} %copy-done.30, bf16[2,32,16,256]{3,2,1,0:T(8,128)(2,1)S(1)} %copy-done.8, ...), custom_call_target="tpu_custom_call" | custom-call | flops 3221225472 | bytes 12582912 | tf_op jit(solution)/shard_map/synthesis/pallas_call | solution.py:159
  (240 shorter events, 114.7 us)
Async XLA Ops:
  0.0 87.3 %collective-permute-start.5 = (bf16[2,64,16,1024]{3,2,1,0:T(8,128)(2,1)}, bf16[2,64,16,1024]{3,2,1,0:T(8,128)(2,1)}, u32[]{:S(2)}, u32[]{:S(2)}) collective-permute-start(bf16[2,64,16,1024]{3,2,1,0:T(8,128)(2,1)} %refs_4_.17), channel_id=1, source_target_pairs={{0,1},{1,0},{2,3},{3,2},{4,5},{5,4},{6,7},{7,6},{8,9},{9,8},{10,11... | collective-permute-start | bytes 12582920 | tf_op jit(solution)/shard_map/ppermute | solution.py:217
  19.0 22.5 %collective-permute-start.1 = (bf16[2,8,16,1024]{3,2,1,0:T(8,128)(2,1)S(1)}, bf16[2,8,16,1024]{3,2,1,0:T(8,128)(2,1)S(1)}, u32[]{:S(2)}, u32[]{:S(2)}) collective-permute-start(bf16[2,8,16,1024]{3,2,1,0:T(8,128)(2,1)S(1)} %collective-permute-done.refs_5_), channel_id=1, source_target_pairs={{0,2},{1,3},{2,4},{3,5},{4,6},{5,7},{6,0},{7,1},{8,10},{9,11},{10,... | collective-permute-start | bytes 1572872 | tf_op jit(solution)/shard_map/ppermute | solution.py:313
  30.2 22.5 %collective-permute-start.3 = (bf16[2,8,16,1024]{3,2,1,0:T(8,128)(2,1)S(1)}, bf16[2,8,16,1024]{3,2,1,0:T(8,128)(2,1)S(1)}, u32[]{:S(2)}, u32[]{:S(2)}) collective-permute-start(bf16[2,8,16,1024]{3,2,1,0:T(8,128)(2,1)S(1)} %get-tuple-element.62), channel_id=1, source_target_pairs={{0,2},{1,3},{2,4},{3,5},{4,6},{5,7},{6,0},{7,1},{8,10},{9,11},{10,... | collective-permute-start | bytes 1572872 | tf_op jit(solution)/shard_map/ppermute | solution.py:313
  41.4 22.5 %collective-permute-start.10 = (bf16[2,8,16,1024]{3,2,1,0:T(8,128)(2,1)S(1)}, bf16[2,8,16,1024]{3,2,1,0:T(8,128)(2,1)S(1)}, u32[]{:S(2)}, u32[]{:S(2)}) collective-permute-start(bf16[2,8,16,1024]{3,2,1,0:T(8,128)(2,1)S(1)} %collective-permute-done.2.refs_5_), channel_id=1, source_target_pairs={{0,2},{1,3},{2,4},{3,5},{4,6},{5,7},{6,0},{7,1},{8,10},{9,11},{10,... | collective-permute-start | bytes 1572872 | tf_op jit(solution)/shard_map/ppermute | solution.py:313
  52.7 22.5 %collective-permute-start.4 = (bf16[2,8,16,1024]{3,2,1,0:T(8,128)(2,1)S(1)}, bf16[2,8,16,1024]{3,2,1,0:T(8,128)(2,1)S(1)}, u32[]{:S(2)}, u32[]{:S(2)}) collective-permute-start(bf16[2,8,16,1024]{3,2,1,0:T(8,128)(2,1)S(1)} %collective-permute-done.1.refs_6_), channel_id=1, source_target_pairs={{0,2},{1,3},{2,4},{3,5},{4,6},{5,7},{6,0},{7,1},{8,10},{9,11},{10,... | collective-permute-start | bytes 1572872 | tf_op jit(solution)/shard_map/ppermute | solution.py:313
  53.7 33.6 %collective-permute-start.6 = (bf16[4,8,16,1024]{3,2,1,0:T(8,128)(2,1)}, bf16[4,8,16,1024]{3,2,1,0:T(8,128)(2,1)}, u32[]{:S(2)}, u32[]{:S(2)}) collective-permute-start(bf16[4,8,16,1024]{3,2,1,0:T(8,128)(2,1)} %pad_maximum_fusion), channel_id=1, source_target_pairs={{0,1},{1,0},{2,3},{3,2},{4,5},{5,4},{6,7},{7,6},{8,9},{9,8},{10,11... | collective-permute-start | bytes 3145736 | tf_op jit(solution)/shard_map/ppermute | solution.py:245
  63.9 22.5 %collective-permute-start.11 = (bf16[2,8,16,1024]{3,2,1,0:T(8,128)(2,1)S(1)}, bf16[2,8,16,1024]{3,2,1,0:T(8,128)(2,1)S(1)}, u32[]{:S(2)}, u32[]{:S(2)}) collective-permute-start(bf16[2,8,16,1024]{3,2,1,0:T(8,128)(2,1)S(1)} %get-tuple-element.67), channel_id=1, source_target_pairs={{0,2},{1,3},{2,4},{3,5},{4,6},{5,7},{6,0},{7,1},{8,10},{9,11},{10,... | collective-permute-start | bytes 1572872 | tf_op jit(solution)/shard_map/ppermute | solution.py:313
  75.2 24.0 %collective-permute-start.17 = (bf16[2,8,16,1024]{3,2,1,0:T(8,128)(2,1)S(1)}, bf16[2,8,16,1024]{3,2,1,0:T(8,128)(2,1)S(1)}, u32[]{:S(2)}, u32[]{:S(2)}) collective-permute-start(bf16[2,8,16,1024]{3,2,1,0:T(8,128)(2,1)S(1)} %collective-permute-done.3.refs_5_), channel_id=1, source_target_pairs={{0,2},{1,3},{2,4},{3,5},{4,6},{5,7},{6,0},{7,1},{8,10},{9,11},{10,... | collective-permute-start | bytes 1572872 | tf_op jit(solution)/shard_map/ppermute | solution.py:313
  86.4 33.7 %collective-permute-start.13 = (bf16[4,8,16,1024]{3,2,1,0:T(8,128)(2,1)}, bf16[4,8,16,1024]{3,2,1,0:T(8,128)(2,1)}, u32[]{:S(2)}, u32[]{:S(2)}) collective-permute-start(bf16[4,8,16,1024]{3,2,1,0:T(8,128)(2,1)} %pad_maximum_fusion.1), channel_id=1, source_target_pairs={{0,1},{1,0},{2,3},{3,2},{4,5},{5,4},{6,7},{7,6},{8,9},{9,8},{10,11... | collective-permute-start | bytes 3145736 | tf_op jit(solution)/shard_map/ppermute | solution.py:245
  87.2 21.7 %collective-permute-start.12 = (bf16[2,8,16,1024]{3,2,1,0:T(8,128)(2,1)S(1)}, bf16[2,8,16,1024]{3,2,1,0:T(8,128)(2,1)}, u32[]{:S(2)}, u32[]{:S(2)}) collective-permute-start(bf16[2,8,16,1024]{3,2,1,0:T(8,128)(2,1)S(1)} %collective-permute-done.10.refs_6_), channel_id=1, source_target_pairs={{0,2},{1,3},{2,4},{3,5},{4,6},{5,7},{6,0},{7,1},{8,10},{9,11},{10,... | collective-permute-start | bytes 1572872 | tf_op jit(solution)/shard_map/ppermute | solution.py:313
  109.0 22.4 %collective-permute-start.24 = (bf16[2,8,16,1024]{3,2,1,0:T(8,128)(2,1)S(1)}, bf16[2,8,16,1024]{3,2,1,0:T(8,128)(2,1)S(1)}, u32[]{:S(2)}, u32[]{:S(2)}) collective-permute-start(bf16[2,8,16,1024]{3,2,1,0:T(8,128)(2,1)S(1)} %collective-permute-done.11.refs_5_), channel_id=1, source_target_pairs={{0,2},{1,3},{2,4},{3,5},{4,6},{5,7},{6,0},{7,1},{8,10},{9,11},{10,... | collective-permute-start | bytes 1572872 | tf_op jit(solution)/shard_map/ppermute | solution.py:313
  109.1 35.4 %collective-permute-start.20 = (bf16[4,8,16,1024]{3,2,1,0:T(8,128)(2,1)S(1)}, bf16[4,8,16,1024]{3,2,1,0:T(8,128)(2,1)S(1)}, u32[]{:S(2)}, u32[]{:S(2)}) collective-permute-start(bf16[4,8,16,1024]{3,2,1,0:T(8,128)(2,1)S(1)} %pad_maximum_fusion.2), channel_id=1, source_target_pairs={{0,1},{1,0},{2,3},{3,2},{4,5},{5,4},{6,7},{7,6},{8,9},{9,8},{10,11... | collective-permute-start | bytes 3145736 | tf_op jit(solution)/shard_map/ppermute | solution.py:245
  120.1 22.5 %collective-permute-start.19 = (bf16[2,8,16,1024]{3,2,1,0:T(8,128)(2,1)S(1)}, bf16[2,8,16,1024]{3,2,1,0:T(8,128)(2,1)S(1)}, u32[]{:S(2)}, u32[]{:S(2)}) collective-permute-start(bf16[2,8,16,1024]{3,2,1,0:T(8,128)(2,1)S(1)} %collective-permute-done.17.refs_6_), channel_id=1, source_target_pairs={{0,2},{1,3},{2,4},{3,5},{4,6},{5,7},{6,0},{7,1},{8,10},{9,11},{10,... | collective-permute-start | bytes 1572872 | tf_op jit(solution)/shard_map/ppermute | solution.py:313
  120.1 22.6 %collective-permute-start.8 = (bf16[2,32,16,256]{3,2,1,0:T(8,128)(2,1)S(1)}, bf16[2,32,16,256]{3,2,1,0:T(8,128)(2,1)S(1)}, u32[]{:S(2)}, u32[]{:S(2)}) collective-permute-start(bf16[2,32,16,256]{3,2,1,0:T(8,128)(2,1)S(1)} %get-tuple-element.65), channel_id=1, source_target_pairs={{0,8},{8,0},{1,9},{9,1},{2,10},{10,2},{3,11},{11,3},{4,12},{12,4},... | collective-permute-start | bytes 1572872 | tf_op jit(solution)/shard_map/ppermute | solution.py:253
  131.3 22.5 %collective-permute-start.25 = (bf16[2,8,16,1024]{3,2,1,0:T(8,128)(2,1)S(1)}, bf16[2,8,16,1024]{3,2,1,0:T(8,128)(2,1)S(1)}, u32[]{:S(2)}, u32[]{:S(2)}) collective-permute-start(bf16[2,8,16,1024]{3,2,1,0:T(8,128)(2,1)S(1)} %copy-done.42), channel_id=1, source_target_pairs={{0,2},{1,3},{2,4},{3,5},{4,6},{5,7},{6,0},{7,1},{8,10},{9,11},{10,... | collective-permute-start | bytes 1572872 | tf_op jit(solution)/shard_map/ppermute | solution.py:313
  142.6 22.5 %collective-permute-start.31 = (bf16[2,8,16,1024]{3,2,1,0:T(8,128)(2,1)S(1)}, bf16[2,8,16,1024]{3,2,1,0:T(8,128)(2,1)S(1)}, u32[]{:S(2)}, u32[]{:S(2)}) collective-permute-start(bf16[2,8,16,1024]{3,2,1,0:T(8,128)(2,1)S(1)} %collective-permute-done.18.refs_5_), channel_id=1, source_target_pairs={{0,2},{1,3},{2,4},{3,5},{4,6},{5,7},{6,0},{7,1},{8,10},{9,11},{10,... | collective-permute-start | bytes 1572872 | tf_op jit(solution)/shard_map/ppermute | solution.py:313
  142.7 22.4 %collective-permute-start.15 = (bf16[2,32,16,256]{3,2,1,0:T(8,128)(2,1)S(1)}, bf16[2,32,16,256]{3,2,1,0:T(8,128)(2,1)S(1)}, u32[]{:S(2)}, u32[]{:S(2)}) collective-permute-start(bf16[2,32,16,256]{3,2,1,0:T(8,128)(2,1)S(1)} %get-tuple-element.70), channel_id=1, source_target_pairs={{0,8},{8,0},{1,9},{9,1},{2,10},{10,2},{3,11},{11,3},{4,12},{12,4},... | collective-permute-start | bytes 1572872 | tf_op jit(solution)/shard_map/ppermute | solution.py:253
  153.8 35.4 %collective-permute-start.27 = (bf16[4,8,16,1024]{3,2,1,0:T(8,128)(2,1)S(1)}, bf16[4,8,16,1024]{3,2,1,0:T(8,128)(2,1)S(1)}, u32[]{:S(2)}, u32[]{:S(2)}) collective-permute-start(bf16[4,8,16,1024]{3,2,1,0:T(8,128)(2,1)S(1)} %pad_maximum_fusion.3), channel_id=1, source_target_pairs={{0,1},{1,0},{2,3},{3,2},{4,5},{5,4},{6,7},{7,6},{8,9},{9,8},{10,11... | collective-permute-start | bytes 3145736 | tf_op jit(solution)/shard_map/ppermute | solution.py:245
  154.5 21.8 %collective-permute-start.26 = (bf16[2,8,16,1024]{3,2,1,0:T(8,128)(2,1)S(1)}, bf16[2,8,16,1024]{3,2,1,0:T(8,128)(2,1)S(1)}, u32[]{:S(2)}, u32[]{:S(2)}) collective-permute-start(bf16[2,8,16,1024]{3,2,1,0:T(8,128)(2,1)S(1)} %collective-permute-done.24.refs_6_), channel_id=1, source_target_pairs={{0,2},{1,3},{2,4},{3,5},{4,6},{5,7},{6,0},{7,1},{8,10},{9,11},{10,... | collective-permute-start | bytes 1572872 | tf_op jit(solution)/shard_map/ppermute | solution.py:313
  165.0 22.5 %collective-permute-start.32 = (bf16[2,8,16,1024]{3,2,1,0:T(8,128)(2,1)S(1)}, bf16[2,8,16,1024]{3,2,1,0:T(8,128)(2,1)S(1)}, u32[]{:S(2)}, u32[]{:S(2)}) collective-permute-start(bf16[2,8,16,1024]{3,2,1,0:T(8,128)(2,1)S(1)} %copy-done.41), channel_id=1, source_target_pairs={{0,2},{1,3},{2,4},{3,5},{4,6},{5,7},{6,0},{7,1},{8,10},{9,11},{10,... | collective-permute-start | bytes 1572872 | tf_op jit(solution)/shard_map/ppermute | solution.py:313
  166.9 51.2 %collective-permute-start.34 = (bf16[4,8,16,1024]{3,2,1,0:T(8,128)(2,1)S(1)}, bf16[4,8,16,1024]{3,2,1,0:T(8,128)(2,1)S(1)}, u32[]{:S(2)}, u32[]{:S(2)}) collective-permute-start(bf16[4,8,16,1024]{3,2,1,0:T(8,128)(2,1)S(1)} %pad_maximum_fusion.4), channel_id=1, source_target_pairs={{0,1},{1,0},{2,3},{3,2},{4,5},{5,4},{6,7},{7,6},{8,9},{9,8},{10,11... | collective-permute-start | bytes 3145736 | tf_op jit(solution)/shard_map/ppermute | solution.py:245
  177.0 21.8 %collective-permute-start.38 = (bf16[2,8,16,1024]{3,2,1,0:T(8,128)(2,1)S(1)}, bf16[2,8,16,1024]{3,2,1,0:T(8,128)(2,1)S(1)}, u32[]{:S(2)}, u32[]{:S(2)}) collective-permute-start(bf16[2,8,16,1024]{3,2,1,0:T(8,128)(2,1)S(1)} %collective-permute-done.25.refs_5_), channel_id=1, source_target_pairs={{0,2},{1,3},{2,4},{3,5},{4,6},{5,7},{6,0},{7,1},{8,10},{9,11},{10,... | collective-permute-start | bytes 1572872 | tf_op jit(solution)/shard_map/ppermute | solution.py:313
  218.1 27.2 %collective-permute-start.41 = (bf16[4,8,16,1024]{3,2,1,0:T(8,128)(2,1)S(1)}, bf16[4,8,16,1024]{3,2,1,0:T(8,128)(2,1)S(1)}, u32[]{:S(2)}, u32[]{:S(2)}) collective-permute-start(bf16[4,8,16,1024]{3,2,1,0:T(8,128)(2,1)S(1)} %pad_maximum_fusion.5), channel_id=1, source_target_pairs={{0,1},{1,0},{2,3},{3,2},{4,5},{5,4},{6,7},{7,6},{8,9},{9,8},{10,11... | collective-permute-start | bytes 3145736 | tf_op jit(solution)/shard_map/ppermute | solution.py:245
  245.1 24.2 %collective-permute-start.48 = (bf16[4,8,16,1024]{3,2,1,0:T(8,128)(2,1)S(1)}, bf16[4,8,16,1024]{3,2,1,0:T(8,128)(2,1)S(1)}, u32[]{:S(2)}, u32[]{:S(2)}) collective-permute-start(bf16[4,8,16,1024]{3,2,1,0:T(8,128)(2,1)S(1)} %pad_maximum_fusion.6), channel_id=1, source_target_pairs={{0,1},{1,0},{2,3},{3,2},{4,5},{5,4},{6,7},{7,6},{8,9},{9,8},{10,11... | collective-permute-start | bytes 3145736 | tf_op jit(solution)/shard_map/ppermute | solution.py:245
  (86 other events, 1319.3 us)

commit v4 on v3

--- a/solution.py
+++ b/solution.py
@@ -147,7 +147,7 @@
 
 
 def synthesis(table, groups, channels, own, beams):
-    times = 8
+    times = 16 if own % 16 == 0 else 8
     in_specs = [pl.BlockSpec(table.shape, lambda i: (0, 0))]
     operands, layout = [], []
     for partials, received in groups:

time: 320 us -> 321 us (level)
  transfers between devices with their start and end apart: 65 -> 65, of which waited for: 33 -> 33; matrix products, arithmetic and copies ran while one was open for 3% -> 3% of each run, Pallas kernels for 17% -> 16%
where the time goes in v4:
time: 321 us
  waiting for transfers between devices  204 us (64%)
  Pallas kernels  60.4 us (19%)
  starting transfers between devices  36 us (11%)
  local copies, waits for them, and re-layouts  13.6 us (4%)
  other arithmetic  5.55 us (2%)
    ppermute x27, waiting for transfers between devices, shards(): got = lax.ppermute(block, 'beam', ring)  183 us
    pallas_call x9, Pallas kernels, beamform(): pl.pallas_call(functools.partial(beamform_kernel, (n, group, time, own, e...  52.9 us
    ppermute x9, starting transfers between devices, over_elements(): lax.ppermute(partials[r], 'elem', [(d, (d + r) % elems) for d in range(el...  13.4 us
    ppermute x9, starting transfers between devices, over_channels(): lax.ppermute(total, 'chan', [(d, (d + q) % chans) for d in range(chans)])  12.2 us
    ppermute x9, waiting for transfers between devices, over_channels(): lax.ppermute(total, 'chan', [(d, (d + q) % chans) for d in range(chans)])  11.3 us
    ppermute x9, waiting for transfers between devices, over_elements(): lax.ppermute(partials[r], 'elem', [(d, (d + r) % elems) for d in range(el...  10.3 us
    ppermute x27, starting transfers between devices, shards(): got = lax.ppermute(block, 'beam', ring)  8.59 us
    unnamed x90, local copies, waits for them, and re-layouts  8.36 us
  transfers between devices with their start and end apart: 65, of which 33 were waited for; matrix products, arithmetic and copies ran while one was open for 3% of the time, Pallas kernels for 16%

profile of v4, /device:TPU:0, one launch (start us, length us, event | category | flops | bytes accessed | tf_op | source)
XLA Modules:
  0.0 320.7 jit_solution(1629538041027671134)
XLA Ops:
  10.5 8.4 %collective-permute-done.refs_5_ = bf16[2,8,16,1024]{3,2,1,0:T(8,128)(2,1)S(1)} collective-permute-done((bf16[2,8,16,1024]{3,2,1,0:T(8,128)(2,1)S(1)}, bf16[2,8,16,1024]{3,2,1,0:T(8,128)(2,1)S(1)}, u32[]{:S(2)}, u32[]{:S(2)}) %collective-permute-start) | collective-permute-done | bytes 524320 | tf_op jit(solution)/shard_map/ppermute | solution.py:313
  19.0 11.2 %collective-permute-done.2.refs_5_ = bf16[2,8,16,1024]{3,2,1,0:T(8,128)(2,1)S(1)} collective-permute-done((bf16[2,8,16,1024]{3,2,1,0:T(8,128)(2,1)S(1)}, bf16[2,8,16,1024]{3,2,1,0:T(8,128)(2,1)S(1)}, u32[]{:S(2)}, u32[]{:S(2)}) %collective-permute-start.2) | collective-permute-done | bytes 524320 | tf_op jit(solution)/shard_map/ppermute | solution.py:313
  30.2 11.2 %collective-permute-done.1.refs_6_ = bf16[2,8,16,1024]{3,2,1,0:T(8,128)(2,1)S(1)} collective-permute-done((bf16[2,8,16,1024]{3,2,1,0:T(8,128)(2,1)S(1)}, bf16[2,8,16,1024]{3,2,1,0:T(8,128)(2,1)S(1)}, u32[]{:S(2)}, u32[]{:S(2)}) %collective-permute-start.1) | collective-permute-done | bytes 524320 | tf_op jit(solution)/shard_map/ppermute | solution.py:313
  41.4 11.2 %collective-permute-done.3.refs_5_ = bf16[2,8,16,1024]{3,2,1,0:T(8,128)(2,1)S(1)} collective-permute-done((bf16[2,8,16,1024]{3,2,1,0:T(8,128)(2,1)S(1)}, bf16[2,8,16,1024]{3,2,1,0:T(8,128)(2,1)S(1)}, u32[]{:S(2)}, u32[]{:S(2)}) %collective-permute-start.3) | collective-permute-done | bytes 524320 | tf_op jit(solution)/shard_map/ppermute | solution.py:313
  53.7 10.2 %collective-permute-done.10.refs_6_ = bf16[2,8,16,1024]{3,2,1,0:T(8,128)(2,1)S(1)} collective-permute-done((bf16[2,8,16,1024]{3,2,1,0:T(8,128)(2,1)S(1)}, bf16[2,8,16,1024]{3,2,1,0:T(8,128)(2,1)S(1)}, u32[]{:S(2)}, u32[]{:S(2)}) %collective-permute-start.10) | collective-permute-done | bytes 524320 | tf_op jit(solution)/shard_map/ppermute | solution.py:313
  63.9 11.2 %collective-permute-done.4.refs_7_ = bf16[2,8,16,1024]{3,2,1,0:T(8,128)(2,1)S(1)} collective-permute-done((bf16[2,8,16,1024]{3,2,1,0:T(8,128)(2,1)S(1)}, bf16[2,8,16,1024]{3,2,1,0:T(8,128)(2,1)S(1)}, u32[]{:S(2)}, u32[]{:S(2)}) %collective-permute-start.4) | collective-permute-done | bytes 524320 | tf_op jit(solution)/shard_map/ppermute | solution.py:313
  76.3 10.0 %collective-permute-done.11.refs_5_ = bf16[2,8,16,1024]{3,2,1,0:T(8,128)(2,1)S(1)} collective-permute-done((bf16[2,8,16,1024]{3,2,1,0:T(8,128)(2,1)S(1)}, bf16[2,8,16,1024]{3,2,1,0:T(8,128)(2,1)S(1)}, u32[]{:S(2)}, u32[]{:S(2)}) %collective-permute-start.11) | collective-permute-done | bytes 524320 | tf_op jit(solution)/shard_map/ppermute | solution.py:313
  92.6 6.4 %beamform.9 = (bf16[2,32,16,256]{3,2,1,0:T(8,128)(2,1)S(1)}, bf16[2,32,16,256]{3,2,1,0:T(8,128)(2,1)S(1)}) custom-call(s32[12]{0:T(128)S(1)} %stack.51.scalars, bf16[2,64,1024,256]{3,2,1,0:T(8,128)(2,1)} %refs_3_.17, bf16[2,64,1024,256]{3,2,1,0:T(8,128)(2,1)} %refs_3_.17, bf16[2,64,1024,256]{3,2,1,0:T(8,128)(2,1)} %refs_3_.17, ...), custom_call_target="tpu_custom_call" | custom-call | tf_op jit(solution)/shard_map/beamform/pallas_call | solution.py:100
  100.7 8.3 %collective-permute-done.12.refs_7_ = bf16[2,8,16,1024]{3,2,1,0:T(8,128)(2,1)} collective-permute-done((bf16[2,8,16,1024]{3,2,1,0:T(8,128)(2,1)S(1)}, bf16[2,8,16,1024]{3,2,1,0:T(8,128)(2,1)}, u32[]{:S(2)}, u32[]{:S(2)}) %collective-permute-start.12) | collective-permute-done | bytes 524320 | tf_op jit(solution)/shard_map/ppermute | solution.py:313
  109.6 10.4 %collective-permute-done.18.refs_5_ = bf16[2,8,16,1024]{3,2,1,0:T(8,128)(2,1)S(1)} collective-permute-done((bf16[2,8,16,1024]{3,2,1,0:T(8,128)(2,1)S(1)}, bf16[2,8,16,1024]{3,2,1,0:T(8,128)(2,1)S(1)}, u32[]{:S(2)}, u32[]{:S(2)}) %collective-permute-start.18) | collective-permute-done | bytes 524320 | tf_op jit(solution)/shard_map/ppermute | solution.py:313
  121.7 6.5 %beamform.10 = (bf16[2,32,16,256]{3,2,1,0:T(8,128)(2,1)S(1)}, bf16[2,32,16,256]{3,2,1,0:T(8,128)(2,1)S(1)}) custom-call(s32[12]{0:T(128)S(1)} %stack.51.scalars, bf16[2,64,1024,256]{3,2,1,0:T(8,128)(2,1)} %refs_3_.17, bf16[2,64,1024,256]{3,2,1,0:T(8,128)(2,1)} %refs_3_.17, bf16[2,64,1024,256]{3,2,1,0:T(8,128)(2,1)} %refs_3_.17, ...), custom_call_target="tpu_custom_call" | custom-call | tf_op jit(solution)/shard_map/beamform/pallas_call | solution.py:100
  131.3 11.2 %collective-permute-done.19.refs_7_ = bf16[2,8,16,1024]{3,2,1,0:T(8,128)(2,1)S(1)} collective-permute-done((bf16[2,8,16,1024]{3,2,1,0:T(8,128)(2,1)S(1)}, bf16[2,8,16,1024]{3,2,1,0:T(8,128)(2,1)S(1)}, u32[]{:S(2)}, u32[]{:S(2)}) %collective-permute-start.19) | collective-permute-done | bytes 524320 | tf_op jit(solution)/shard_map/ppermute | solution.py:313
  146.1 7.7 %collective-permute-done.25.refs_5_ = bf16[2,8,16,1024]{3,2,1,0:T(8,128)(2,1)S(1)} collective-permute-done((bf16[2,8,16,1024]{3,2,1,0:T(8,128)(2,1)S(1)}, bf16[2,8,16,1024]{3,2,1,0:T(8,128)(2,1)S(1)}, u32[]{:S(2)}, u32[]{:S(2)}) %collective-permute-start.25) | collective-permute-done | bytes 524320 | tf_op jit(solution)/shard_map/ppermute | solution.py:313
  155.1 6.3 %beamform.11 = (bf16[2,32,16,256]{3,2,1,0:T(8,128)(2,1)S(1)}, bf16[2,32,16,256]{3,2,1,0:T(8,128)(2,1)S(1)}) custom-call(s32[12]{0:T(128)S(1)} %stack.51.scalars, bf16[2,64,1024,256]{3,2,1,0:T(8,128)(2,1)} %refs_3_.17, bf16[2,64,1024,256]{3,2,1,0:T(8,128)(2,1)} %refs_3_.17, bf16[2,64,1024,256]{3,2,1,0:T(8,128)(2,1)} %refs_3_.17, ...), custom_call_target="tpu_custom_call" | custom-call | tf_op jit(solution)/shard_map/beamform/pallas_call | solution.py:100
  167.0 9.3 %collective-permute-done.26.refs_7_ = bf16[2,8,16,1024]{3,2,1,0:T(8,128)(2,1)S(1)} collective-permute-done((bf16[2,8,16,1024]{3,2,1,0:T(8,128)(2,1)S(1)}, bf16[2,8,16,1024]{3,2,1,0:T(8,128)(2,1)S(1)}, u32[]{:S(2)}, u32[]{:S(2)}) %collective-permute-start.26) | collective-permute-done | bytes 524320 | tf_op jit(solution)/shard_map/ppermute | solution.py:313
  177.0 10.5 %collective-permute-done.32.refs_5_ = bf16[2,8,16,1024]{3,2,1,0:T(8,128)(2,1)S(1)} collective-permute-done((bf16[2,8,16,1024]{3,2,1,0:T(8,128)(2,1)S(1)}, bf16[2,8,16,1024]{3,2,1,0:T(8,128)(2,1)S(1)}, u32[]{:S(2)}, u32[]{:S(2)}) %collective-permute-start.32) | collective-permute-done | bytes 524320 | tf_op jit(solution)/shard_map/ppermute | solution.py:313
  189.9 6.3 %beamform.12 = (bf16[2,32,16,256]{3,2,1,0:T(8,128)(2,1)S(1)}, bf16[2,32,16,256]{3,2,1,0:T(8,128)(2,1)S(1)}) custom-call(s32[12]{0:T(128)S(1)} %stack.51.scalars, bf16[2,64,1024,256]{3,2,1,0:T(8,128)(2,1)} %refs_3_.17, bf16[2,64,1024,256]{3,2,1,0:T(8,128)(2,1)} %refs_3_.17, bf16[2,64,1024,256]{3,2,1,0:T(8,128)(2,1)} %refs_3_.17, ...), custom_call_target="tpu_custom_call" | custom-call | tf_op jit(solution)/shard_map/beamform/pallas_call | solution.py:100
  202.6 7.4 %collective-permute-done.33.refs_7_ = bf16[2,8,16,1024]{3,2,1,0:T(8,128)(2,1)S(1)} collective-permute-done((bf16[2,8,16,1024]{3,2,1,0:T(8,128)(2,1)S(1)}, bf16[2,8,16,1024]{3,2,1,0:T(8,128)(2,1)S(1)}, u32[]{:S(2)}, u32[]{:S(2)}) %collective-permute-start.33) | collective-permute-done | bytes 524320 | tf_op jit(solution)/shard_map/ppermute | solution.py:313
  218.1 6.3 %beamform.13 = (bf16[2,32,16,256]{3,2,1,0:T(8,128)(2,1)S(1)}, bf16[2,32,16,256]{3,2,1,0:T(8,128)(2,1)S(1)}) custom-call(s32[12]{0:T(128)S(1)} %stack.51.scalars, bf16[2,64,1024,256]{3,2,1,0:T(8,128)(2,1)} %refs_3_.17, bf16[2,64,1024,256]{3,2,1,0:T(8,128)(2,1)} %refs_3_.17, bf16[2,64,1024,256]{3,2,1,0:T(8,128)(2,1)} %refs_3_.17, ...), custom_call_target="tpu_custom_call" | custom-call | tf_op jit(solution)/shard_map/beamform/pallas_call | solution.py:100
  230.7 7.4 %collective-permute-done.40.refs_7_ = bf16[2,8,16,1024]{3,2,1,0:T(8,128)(2,1)S(1)} collective-permute-done((bf16[2,8,16,1024]{3,2,1,0:T(8,128)(2,1)S(1)}, bf16[2,8,16,1024]{3,2,1,0:T(8,128)(2,1)S(1)}, u32[]{:S(2)}, u32[]{:S(2)}) %collective-permute-start.40) | collective-permute-done | bytes 524320 | tf_op jit(solution)/shard_map/ppermute | solution.py:313
  245.2 6.3 %beamform.14 = (bf16[2,32,16,256]{3,2,1,0:T(8,128)(2,1)S(1)}, bf16[2,32,16,256]{3,2,1,0:T(8,128)(2,1)S(1)}) custom-call(s32[12]{0:T(128)S(1)} %stack.51.scalars, bf16[2,64,1024,256]{3,2,1,0:T(8,128)(2,1)} %refs_3_.17, bf16[2,64,1024,256]{3,2,1,0:T(8,128)(2,1)} %refs_3_.17, bf16[2,64,1024,256]{3,2,1,0:T(8,128)(2,1)} %refs_3_.17, ...), custom_call_target="tpu_custom_call" | custom-call | tf_op jit(solution)/shard_map/beamform/pallas_call | solution.py:100
  253.4 6.7 %collective-permute-done.47.refs_7_ = bf16[2,8,16,1024]{3,2,1,0:T(8,128)(2,1)S(1)} collective-permute-done((bf16[2,8,16,1024]{3,2,1,0:T(8,128)(2,1)S(1)}, bf16[2,8,16,1024]{3,2,1,0:T(8,128)(2,1)S(1)}, u32[]{:S(2)}, u32[]{:S(2)}) %collective-permute-start.47) | collective-permute-done | bytes 524320 | tf_op jit(solution)/shard_map/ppermute | solution.py:313
  270.9 7.0 %beamform.15 = (bf16[2,32,16,256]{3,2,1,0:T(8,128)(2,1)S(1)}, bf16[2,32,16,256]{3,2,1,0:T(8,128)(2,1)}) custom-call(s32[12]{0:T(128)S(1)} %stack.51.scalars, bf16[2,64,1024,256]{3,2,1,0:T(8,128)(2,1)} %refs_3_.17, bf16[2,64,1024,256]{3,2,1,0:T(8,128)(2,1)} %refs_3_.17, bf16[2,64,1024,256]{3,2,1,0:T(8,128)(2,1)} %refs_3_.17, ...), custom_call_target="tpu_custom_call" | custom-call | tf_op jit(solution)/shard_map/beamform/pallas_call | solution.py:100
  313.3 7.5 %synthesis.1 = f32[128,32,256]{2,1,0:T(8,128)} custom-call(bf16[768,256]{1,0:T(8,128)(2,1)S(1)} %pad_maximum_fusion.8.table, bf16[2,32,16,256]{3,2,1,0:T(8,128)(2,1)S(1)} %copy-done.4, bf16[2,32,16,256]{3,2,1,0:T(8,128)(2,1)S(1)} %copy-done.6, bf16[32,16,256]{2,1,0:T(8,128)(2,1)S(1)} %copy-done.30, bf16[2,32,16,256]{3,2,1,0:T(8,128)(2,1)S(1)} %copy-done.8, ...), custom_call_target="tpu_custom_call" | custom-call | flops 3221225472 | bytes 12582912 | tf_op jit(solution)/shard_map/synthesis/pallas_call | solution.py:159
  (240 shorter events, 114.7 us)
Async XLA Ops:
  0.0 87.3 %collective-permute-start.5 = (bf16[2,64,16,1024]{3,2,1,0:T(8,128)(2,1)}, bf16[2,64,16,1024]{3,2,1,0:T(8,128)(2,1)}, u32[]{:S(2)}, u32[]{:S(2)}) collective-permute-start(bf16[2,64,16,1024]{3,2,1,0:T(8,128)(2,1)} %refs_4_.17), channel_id=1, source_target_pairs={{0,1},{1,0},{2,3},{3,2},{4,5},{5,4},{6,7},{7,6},{8,9},{9,8},{10,11... | collective-permute-start | bytes 12582920 | tf_op jit(solution)/shard_map/ppermute | solution.py:217
  19.0 22.5 %collective-permute-start.1 = (bf16[2,8,16,1024]{3,2,1,0:T(8,128)(2,1)S(1)}, bf16[2,8,16,1024]{3,2,1,0:T(8,128)(2,1)S(1)}, u32[]{:S(2)}, u32[]{:S(2)}) collective-permute-start(bf16[2,8,16,1024]{3,2,1,0:T(8,128)(2,1)S(1)} %collective-permute-done.refs_5_), channel_id=1, source_target_pairs={{0,2},{1,3},{2,4},{3,5},{4,6},{5,7},{6,0},{7,1},{8,10},{9,11},{10,... | collective-permute-start | bytes 1572872 | tf_op jit(solution)/shard_map/ppermute | solution.py:313
  30.2 22.5 %collective-permute-start.3 = (bf16[2,8,16,1024]{3,2,1,0:T(8,128)(2,1)S(1)}, bf16[2,8,16,1024]{3,2,1,0:T(8,128)(2,1)S(1)}, u32[]{:S(2)}, u32[]{:S(2)}) collective-permute-start(bf16[2,8,16,1024]{3,2,1,0:T(8,128)(2,1)S(1)} %get-tuple-element.62), channel_id=1, source_target_pairs={{0,2},{1,3},{2,4},{3,5},{4,6},{5,7},{6,0},{7,1},{8,10},{9,11},{10,... | collective-permute-start | bytes 1572872 | tf_op jit(solution)/shard_map/ppermute | solution.py:313
  41.4 22.5 %collective-permute-start.10 = (bf16[2,8,16,1024]{3,2,1,0:T(8,128)(2,1)S(1)}, bf16[2,8,16,1024]{3,2,1,0:T(8,128)(2,1)S(1)}, u32[]{:S(2)}, u32[]{:S(2)}) collective-permute-start(bf16[2,8,16,1024]{3,2,1,0:T(8,128)(2,1)S(1)} %collective-permute-done.2.refs_5_), channel_id=1, source_target_pairs={{0,2},{1,3},{2,4},{3,5},{4,6},{5,7},{6,0},{7,1},{8,10},{9,11},{10,... | collective-permute-start | bytes 1572872 | tf_op jit(solution)/shard_map/ppermute | solution.py:313
  52.7 22.5 %collective-permute-start.4 = (bf16[2,8,16,1024]{3,2,1,0:T(8,128)(2,1)S(1)}, bf16[2,8,16,1024]{3,2,1,0:T(8,128)(2,1)S(1)}, u32[]{:S(2)}, u32[]{:S(2)}) collective-permute-start(bf16[2,8,16,1024]{3,2,1,0:T(8,128)(2,1)S(1)} %collective-permute-done.1.refs_6_), channel_id=1, source_target_pairs={{0,2},{1,3},{2,4},{3,5},{4,6},{5,7},{6,0},{7,1},{8,10},{9,11},{10,... | collective-permute-start | bytes 1572872 | tf_op jit(solution)/shard_map/ppermute | solution.py:313
  53.7 33.6 %collective-permute-start.6 = (bf16[4,8,16,1024]{3,2,1,0:T(8,128)(2,1)}, bf16[4,8,16,1024]{3,2,1,0:T(8,128)(2,1)}, u32[]{:S(2)}, u32[]{:S(2)}) collective-permute-start(bf16[4,8,16,1024]{3,2,1,0:T(8,128)(2,1)} %pad_maximum_fusion), channel_id=1, source_target_pairs={{0,1},{1,0},{2,3},{3,2},{4,5},{5,4},{6,7},{7,6},{8,9},{9,8},{10,11... | collective-permute-start | bytes 3145736 | tf_op jit(solution)/shard_map/ppermute | solution.py:245
  63.9 22.5 %collective-permute-start.11 = (bf16[2,8,16,1024]{3,2,1,0:T(8,128)(2,1)S(1)}, bf16[2,8,16,1024]{3,2,1,0:T(8,128)(2,1)S(1)}, u32[]{:S(2)}, u32[]{:S(2)}) collective-permute-start(bf16[2,8,16,1024]{3,2,1,0:T(8,128)(2,1)S(1)} %get-tuple-element.67), channel_id=1, source_target_pairs={{0,2},{1,3},{2,4},{3,5},{4,6},{5,7},{6,0},{7,1},{8,10},{9,11},{10,... | collective-permute-start | bytes 1572872 | tf_op jit(solution)/shard_map/ppermute | solution.py:313
  75.2 24.0 %collective-permute-start.17 = (bf16[2,8,16,1024]{3,2,1,0:T(8,128)(2,1)S(1)}, bf16[2,8,16,1024]{3,2,1,0:T(8,128)(2,1)S(1)}, u32[]{:S(2)}, u32[]{:S(2)}) collective-permute-start(bf16[2,8,16,1024]{3,2,1,0:T(8,128)(2,1)S(1)} %collective-permute-done.3.refs_5_), channel_id=1, source_target_pairs={{0,2},{1,3},{2,4},{3,5},{4,6},{5,7},{6,0},{7,1},{8,10},{9,11},{10,... | collective-permute-start | bytes 1572872 | tf_op jit(solution)/shard_map/ppermute | solution.py:313
  86.4 33.7 %collective-permute-start.13 = (bf16[4,8,16,1024]{3,2,1,0:T(8,128)(2,1)}, bf16[4,8,16,1024]{3,2,1,0:T(8,128)(2,1)}, u32[]{:S(2)}, u32[]{:S(2)}) collective-permute-start(bf16[4,8,16,1024]{3,2,1,0:T(8,128)(2,1)} %pad_maximum_fusion.1), channel_id=1, source_target_pairs={{0,1},{1,0},{2,3},{3,2},{4,5},{5,4},{6,7},{7,6},{8,9},{9,8},{10,11... | collective-permute-start | bytes 3145736 | tf_op jit(solution)/shard_map/ppermute | solution.py:245
  87.2 21.7 %collective-permute-start.12 = (bf16[2,8,16,1024]{3,2,1,0:T(8,128)(2,1)S(1)}, bf16[2,8,16,1024]{3,2,1,0:T(8,128)(2,1)}, u32[]{:S(2)}, u32[]{:S(2)}) collective-permute-start(bf16[2,8,16,1024]{3,2,1,0:T(8,128)(2,1)S(1)} %collective-permute-done.10.refs_6_), channel_id=1, source_target_pairs={{0,2},{1,3},{2,4},{3,5},{4,6},{5,7},{6,0},{7,1},{8,10},{9,11},{10,... | collective-permute-start | bytes 1572872 | tf_op jit(solution)/shard_map/ppermute | solution.py:313
  109.0 22.4 %collective-permute-start.24 = (bf16[2,8,16,1024]{3,2,1,0:T(8,128)(2,1)S(1)}, bf16[2,8,16,1024]{3,2,1,0:T(8,128)(2,1)S(1)}, u32[]{:S(2)}, u32[]{:S(2)}) collective-permute-start(bf16[2,8,16,1024]{3,2,1,0:T(8,128)(2,1)S(1)} %collective-permute-done.11.refs_5_), channel_id=1, source_target_pairs={{0,2},{1,3},{2,4},{3,5},{4,6},{5,7},{6,0},{7,1},{8,10},{9,11},{10,... | collective-permute-start | bytes 1572872 | tf_op jit(solution)/shard_map/ppermute | solution.py:313
  109.1 35.4 %collective-permute-start.20 = (bf16[4,8,16,1024]{3,2,1,0:T(8,128)(2,1)S(1)}, bf16[4,8,16,1024]{3,2,1,0:T(8,128)(2,1)S(1)}, u32[]{:S(2)}, u32[]{:S(2)}) collective-permute-start(bf16[4,8,16,1024]{3,2,1,0:T(8,128)(2,1)S(1)} %pad_maximum_fusion.2), channel_id=1, source_target_pairs={{0,1},{1,0},{2,3},{3,2},{4,5},{5,4},{6,7},{7,6},{8,9},{9,8},{10,11... | collective-permute-start | bytes 3145736 | tf_op jit(solution)/shard_map/ppermute | solution.py:245
  120.1 22.5 %collective-permute-start.19 = (bf16[2,8,16,1024]{3,2,1,0:T(8,128)(2,1)S(1)}, bf16[2,8,16,1024]{3,2,1,0:T(8,128)(2,1)S(1)}, u32[]{:S(2)}, u32[]{:S(2)}) collective-permute-start(bf16[2,8,16,1024]{3,2,1,0:T(8,128)(2,1)S(1)} %collective-permute-done.17.refs_6_), channel_id=1, source_target_pairs={{0,2},{1,3},{2,4},{3,5},{4,6},{5,7},{6,0},{7,1},{8,10},{9,11},{10,... | collective-permute-start | bytes 1572872 | tf_op jit(solution)/shard_map/ppermute | solution.py:313
  120.1 22.6 %collective-permute-start.8 = (bf16[2,32,16,256]{3,2,1,0:T(8,128)(2,1)S(1)}, bf16[2,32,16,256]{3,2,1,0:T(8,128)(2,1)S(1)}, u32[]{:S(2)}, u32[]{:S(2)}) collective-permute-start(bf16[2,32,16,256]{3,2,1,0:T(8,128)(2,1)S(1)} %get-tuple-element.65), channel_id=1, source_target_pairs={{0,8},{8,0},{1,9},{9,1},{2,10},{10,2},{3,11},{11,3},{4,12},{12,4},... | collective-permute-start | bytes 1572872 | tf_op jit(solution)/shard_map/ppermute | solution.py:253
  131.3 22.5 %collective-permute-start.25 = (bf16[2,8,16,1024]{3,2,1,0:T(8,128)(2,1)S(1)}, bf16[2,8,16,1024]{3,2,1,0:T(8,128)(2,1)S(1)}, u32[]{:S(2)}, u32[]{:S(2)}) collective-permute-start(bf16[2,8,16,1024]{3,2,1,0:T(8,128)(2,1)S(1)} %copy-done.42), channel_id=1, source_target_pairs={{0,2},{1,3},{2,4},{3,5},{4,6},{5,7},{6,0},{7,1},{8,10},{9,11},{10,... | collective-permute-start | bytes 1572872 | tf_op jit(solution)/shard_map/ppermute | solution.py:313
  142.6 22.5 %collective-permute-start.31 = (bf16[2,8,16,1024]{3,2,1,0:T(8,128)(2,1)S(1)}, bf16[2,8,16,1024]{3,2,1,0:T(8,128)(2,1)S(1)}, u32[]{:S(2)}, u32[]{:S(2)}) collective-permute-start(bf16[2,8,16,1024]{3,2,1,0:T(8,128)(2,1)S(1)} %collective-permute-done.18.refs_5_), channel_id=1, source_target_pairs={{0,2},{1,3},{2,4},{3,5},{4,6},{5,7},{6,0},{7,1},{8,10},{9,11},{10,... | collective-permute-start | bytes 1572872 | tf_op jit(solution)/shard_map/ppermute | solution.py:313
  142.7 22.4 %collective-permute-start.15 = (bf16[2,32,16,256]{3,2,1,0:T(8,128)(2,1)S(1)}, bf16[2,32,16,256]{3,2,1,0:T(8,128)(2,1)S(1)}, u32[]{:S(2)}, u32[]{:S(2)}) collective-permute-start(bf16[2,32,16,256]{3,2,1,0:T(8,128)(2,1)S(1)} %get-tuple-element.70), channel_id=1, source_target_pairs={{0,8},{8,0},{1,9},{9,1},{2,10},{10,2},{3,11},{11,3},{4,12},{12,4},... | collective-permute-start | bytes 1572872 | tf_op jit(solution)/shard_map/ppermute | solution.py:253
  153.8 35.4 %collective-permute-start.27 = (bf16[4,8,16,1024]{3,2,1,0:T(8,128)(2,1)S(1)}, bf16[4,8,16,1024]{3,2,1,0:T(8,128)(2,1)S(1)}, u32[]{:S(2)}, u32[]{:S(2)}) collective-permute-start(bf16[4,8,16,1024]{3,2,1,0:T(8,128)(2,1)S(1)} %pad_maximum_fusion.3), channel_id=1, source_target_pairs={{0,1},{1,0},{2,3},{3,2},{4,5},{5,4},{6,7},{7,6},{8,9},{9,8},{10,11... | collective-permute-start | bytes 3145736 | tf_op jit(solution)/shard_map/ppermute | solution.py:245
  154.5 21.8 %collective-permute-start.26 = (bf16[2,8,16,1024]{3,2,1,0:T(8,128)(2,1)S(1)}, bf16[2,8,16,1024]{3,2,1,0:T(8,128)(2,1)S(1)}, u32[]{:S(2)}, u32[]{:S(2)}) collective-permute-start(bf16[2,8,16,1024]{3,2,1,0:T(8,128)(2,1)S(1)} %collective-permute-done.24.refs_6_), channel_id=1, source_target_pairs={{0,2},{1,3},{2,4},{3,5},{4,6},{5,7},{6,0},{7,1},{8,10},{9,11},{10,... | collective-permute-start | bytes 1572872 | tf_op jit(solution)/shard_map/ppermute | solution.py:313
  165.0 22.5 %collective-permute-start.32 = (bf16[2,8,16,1024]{3,2,1,0:T(8,128)(2,1)S(1)}, bf16[2,8,16,1024]{3,2,1,0:T(8,128)(2,1)S(1)}, u32[]{:S(2)}, u32[]{:S(2)}) collective-permute-start(bf16[2,8,16,1024]{3,2,1,0:T(8,128)(2,1)S(1)} %copy-done.41), channel_id=1, source_target_pairs={{0,2},{1,3},{2,4},{3,5},{4,6},{5,7},{6,0},{7,1},{8,10},{9,11},{10,... | collective-permute-start | bytes 1572872 | tf_op jit(solution)/shard_map/ppermute | solution.py:313
  166.9 51.2 %collective-permute-start.34 = (bf16[4,8,16,1024]{3,2,1,0:T(8,128)(2,1)S(1)}, bf16[4,8,16,1024]{3,2,1,0:T(8,128)(2,1)S(1)}, u32[]{:S(2)}, u32[]{:S(2)}) collective-permute-start(bf16[4,8,16,1024]{3,2,1,0:T(8,128)(2,1)S(1)} %pad_maximum_fusion.4), channel_id=1, source_target_pairs={{0,1},{1,0},{2,3},{3,2},{4,5},{5,4},{6,7},{7,6},{8,9},{9,8},{10,11... | collective-permute-start | bytes 3145736 | tf_op jit(solution)/shard_map/ppermute | solution.py:245
  177.0 21.8 %collective-permute-start.38 = (bf16[2,8,16,1024]{3,2,1,0:T(8,128)(2,1)S(1)}, bf16[2,8,16,1024]{3,2,1,0:T(8,128)(2,1)S(1)}, u32[]{:S(2)}, u32[]{:S(2)}) collective-permute-start(bf16[2,8,16,1024]{3,2,1,0:T(8,128)(2,1)S(1)} %collective-permute-done.25.refs_5_), channel_id=1, source_target_pairs={{0,2},{1,3},{2,4},{3,5},{4,6},{5,7},{6,0},{7,1},{8,10},{9,11},{10,... | collective-permute-start | bytes 1572872 | tf_op jit(solution)/shard_map/ppermute | solution.py:313
  218.1 27.2 %collective-permute-start.41 = (bf16[4,8,16,1024]{3,2,1,0:T(8,128)(2,1)S(1)}, bf16[4,8,16,1024]{3,2,1,0:T(8,128)(2,1)S(1)}, u32[]{:S(2)}, u32[]{:S(2)}) collective-permute-start(bf16[4,8,16,1024]{3,2,1,0:T(8,128)(2,1)S(1)} %pad_maximum_fusion.5), channel_id=1, source_target_pairs={{0,1},{1,0},{2,3},{3,2},{4,5},{5,4},{6,7},{7,6},{8,9},{9,8},{10,11... | collective-permute-start | bytes 3145736 | tf_op jit(solution)/shard_map/ppermute | solution.py:245
  245.1 24.2 %collective-permute-start.48 = (bf16[4,8,16,1024]{3,2,1,0:T(8,128)(2,1)S(1)}, bf16[4,8,16,1024]{3,2,1,0:T(8,128)(2,1)S(1)}, u32[]{:S(2)}, u32[]{:S(2)}) collective-permute-start(bf16[4,8,16,1024]{3,2,1,0:T(8,128)(2,1)S(1)} %pad_maximum_fusion.6), channel_id=1, source_target_pairs={{0,1},{1,0},{2,3},{3,2},{4,5},{5,4},{6,7},{7,6},{8,9},{9,8},{10,11... | collective-permute-start | bytes 3145736 | tf_op jit(solution)/shard_map/ppermute | solution.py:245
  (86 other events, 1319.3 us)
